TPU v7x, 512 devices: a whole 4x4x16 slice. The times are simulated.
512 devices in a mesh: sec: 4 (over x), dom: 128 (over y, z, core).
Axes of the slice: x: 4, y: 4, z: 16, core: 2. Of those that a mesh axis runs over, the one named last changes fastest.
Arguments:
- state: float32 [4, 30, 4096, 128], P('sec', None, 'dom'), may hold values from -6 to 6
- surface_frac: float32 [4, 4096, 128], P('sec', 'dom'), may hold values from 0.2 to 1
- diffusivity: float32 [4, 30], P('sec'), may hold values from 0.05 to 0.24
- column_ops: float32 [4, 30, 30], P('sec'), may hold values from -1 to 1
- remap_weights: float32 [4, 1024, 128, 128], P('sec', 'dom'), may hold values from -0.5 to 0.5
- flux_owner: int32 [4, 4096, 1], P('sec', 'dom'), may hold values from 0 to 127; in each aligned block of 32 rows (0 to 31, 32 to 63, ..., all dimensions but the last counted through in order) at most 2 rows name the same one
- flux_row: int32 [4, 4096], P('sec', 'dom'), may hold values from 0 to 31
- flux_block: int32 [4, 4096], P('sec', 'dom'), may hold values from 0 to 7
- runoff_owner: int32 [4, 4096, 1], P('sec', 'dom'), may hold values from 0 to 127; in each aligned block of 32 rows (0 to 31, 32 to 63, ..., all dimensions but the last counted through in order) at most 2 rows name the same one
- runoff_row: int32 [4, 4096], P('sec', 'dom'), may hold values from 0 to 31
- runoff_block: int32 [4, 4096], P('sec', 'dom'), may hold values from 0 to 7
- river_store: float32 [4, 4096, 128], P('sec', 'dom'), may hold values from -6 to 6
Outputs:
- state_out: float32 [4, 30, 4096, 128], P('sec', None, 'dom')
- river_out: float32 [4, 4096, 128], P('sec', 'dom')
Inputs may be any that keep to these rules, and one draw needn't show every extreme that they name: `flux_owner`: among the 32 rows of one device no owner is named by more than 2 rows, a bound that some block reaches. `runoff_owner`: among the 32 rows of one device no owner is named by more than 2 rows, a bound that some block reaches.
All inputs are finite; a program needn't handle non-finite values.
Results may differ from a plain program's by a relative error of at most 0.0003.
Values sent between devices are 32-bit elements; how exact they have to be, the bound alone decides.
A program may use at most 64 MiB of HBM per device.

v0:
```python
import jax
import jax.numpy as jnp
from jax import lax
from jax.sharding import PartitionSpec as P

FIELDS = 4
STEPS = 2


HIGHEST_PRECISION = lax.Precision.HIGHEST


def partner(value, axis, stride):
    mask = 2**stride
    pairs = [(source, source ^ mask) for source in range(lax.axis_size(axis))]
    return lax.ppermute(value, axis, pairs)


def with_halo(cells, sides, width):
    for axis, dim in sides:
        count = lax.axis_size(axis)
        ends = count - 1
        head = lax.slice_in_dim(cells, 0, width, axis=dim)
        tail = lax.slice_in_dim(cells, cells.shape[dim] - width, cells.shape[dim], axis=dim)
        cells = jnp.concatenate(
            [
                lax.ppermute(tail, axis, [(i, (i + 1) % count) for i in range(ends)]),
                cells,
                lax.ppermute(head, axis, [((i + 1) % count, i) for i in range(ends)]),
            ],
            axis=dim,
        )
    return cells


def pack_slots(terms, owner, target, owner_count, slot_count):
    onehot = (owner[:, None] == jnp.arange(owner_count, dtype=jnp.int32)[None, :]).astype(jnp.int32)
    slot_index = jnp.sum(jnp.cumsum(onehot, axis=0) * onehot, axis=1) - 1
    buffer = jnp.zeros((owner_count, slot_count) + terms.shape[1:], jnp.float32)
    buffer = buffer.at[owner, slot_index].set(terms, mode="drop")
    labels = (
        jnp.full((owner_count, slot_count), -1, jnp.int32)
        .at[owner, slot_index]
        .set(target, mode="drop")
    )
    return (buffer, labels)


def row_selector(labels, row_count):
    return (labels.reshape(-1)[:, None] == jnp.arange(row_count, dtype=jnp.int32)[None, :]).astype(
        jnp.float32
    )


def place_flux(buffer, labels, row_count):
    flattened = buffer.reshape((-1,) + buffer.shape[2:])
    return jnp.einsum(
        "sr,sfd->frd", row_selector(labels, row_count), flattened, precision=HIGHEST_PRECISION
    )


def place_runoff(buffer, labels, row_count):
    flattened = buffer.reshape((-1, buffer.shape[2]))
    return jnp.einsum(
        "sr,sd->rd", row_selector(labels, row_count), flattened, precision=HIGHEST_PRECISION
    )


def column_update(field, forcing, fraction, coefficients, operator):
    interior = field[:, 1:-1]
    laplacian = (
        field[:, 2:]
        + field[:, :-2]
        + jnp.roll(interior, 1, 2)
        + jnp.roll(interior, -1, 2)
        - 4.0 * interior
    )
    updated = interior + coefficients[:, None, None] * laplacian
    updated = updated.at[: forcing.shape[0]].add(fraction[None] * forcing)
    return jnp.einsum("kl,lrc->krc", operator, updated, precision=HIGHEST_PRECISION)


def shards(
    state,
    surface_frac,
    diffusivity,
    column_ops,
    remap_weights,
    flux_owner,
    flux_row,
    flux_block,
    runoff_owner,
    runoff_row,
    runoff_block,
    river_store,
):
    column = state[0]
    row_count = column.shape[1]
    owner_count = lax.axis_size("dom")
    slot_count = max(2, 2 * row_count // owner_count)
    weight_table = remap_weights[0]
    block_count = weight_table.shape[0]
    products = jnp.einsum(
        "frc,wcd->rwfd", column[:FIELDS], weight_table, precision=HIGHEST_PRECISION
    )
    block_grid = jnp.arange(block_count, dtype=jnp.int32)[None, :]
    flux_choice = (flux_block[0][:, None] == block_grid).astype(jnp.float32)
    runoff_choice = (runoff_block[0][:, None] == block_grid).astype(jnp.float32)
    flux_terms = jnp.einsum("rw,rwfd->rfd", flux_choice, products, precision=HIGHEST_PRECISION)
    runoff_terms = jnp.einsum(
        "rw,rwd->rd", runoff_choice, products[:, :, 0], precision=HIGHEST_PRECISION
    )
    flux_buffer, flux_labels = pack_slots(
        flux_terms, flux_owner[0, :, 0], flux_row[0], owner_count, slot_count
    )
    runoff_buffer, runoff_labels = pack_slots(
        runoff_terms, runoff_owner[0, :, 0], runoff_row[0], owner_count, slot_count
    )
    moved = partner((flux_buffer, flux_labels), "sec", 1)
    arrived = (
        lax.all_to_all(moved[0], "dom", split_axis=0, concat_axis=0, tiled=True),
        lax.all_to_all(moved[1], "dom", split_axis=0, concat_axis=0, tiled=True),
    )
    imported = place_flux(arrived[0], arrived[1], row_count)
    runoff_arrived = (
        lax.all_to_all(runoff_buffer, "dom", split_axis=0, concat_axis=0, tiled=True),
        lax.all_to_all(runoff_labels, "dom", split_axis=0, concat_axis=0, tiled=True),
    )
    river_in = place_runoff(runoff_arrived[0], runoff_arrived[1], row_count)
    fraction = surface_frac[0]
    coefficients = diffusivity[0]
    operator = column_ops[0]
    field = column
    for step_number in range(STEPS):
        padded = with_halo(field, (("dom", 1),), 1)
        field = column_update(padded, imported, fraction, coefficients, operator)
    return (field[None], river_store + river_in[None])


def solution(mesh):
    in_specs = (
        P("sec", None, "dom", None),
        P("sec", "dom", None),
        P("sec", None),
        P("sec", None, None),
        P("sec", "dom", None, None),
        P("sec", "dom", None),
        P("sec", "dom"),
        P("sec", "dom"),
        P("sec", "dom", None),
        P("sec", "dom"),
        P("sec", "dom"),
        P("sec", "dom", None),
    )
    out_specs = (P("sec", None, "dom", None), P("sec", "dom", None))
    return jax.shard_map(shards, mesh=mesh, in_specs=in_specs, out_specs=out_specs, check_vma=False)
```

profile of v0, /device:TPU:1, one launch (start us, length us, event | category | flops | bytes accessed | tf_op | source)
XLA Modules:
  0.0 150.4 jit_solution(16928727897973989777)
XLA Ops:
  0.7 0.7 copy-done.6
  1.7 0.7 copy-done.7
  2.7 0.6 copy-done.9
  3.3 2.0 %scatter_fusion.1 = s32[128,2]{0,1:T(2,128)S(1)} fusion(s32[128,2]{0,1:T(2,128)S(1)} %broadcast.143.clone, s32[32]{0:T(128)S(1)} %get-tuple-element.46, s32[32]{0:T(128)S(1)} %bitcast.115), kind=kCustom, calls=%fused_computation.1 | custom fusion | bytes 640 | tf_op jit(solution)/shard_map/scatter | solution.py:44
  5.3 5.5 %collective-permute-start.3 = (s32[128,2]{0,1:T(2,128)S(1)}, s32[128,2]{0,1:T(2,128)S(1)}, u32[]{:S(2)}, u32[]{:S(2)}) collective-permute-start(s32[128,2]{0,1:T(2,128)S(1)} %scatter_fusion.1), channel_id=1, source_target_pairs={{0,256},{128,384},{256,0},{384,128},{1,257},{129,385},{257,1},{385... | collective-permute-start | bytes 3080 | tf_op jit(solution)/shard_map/ppermute | solution.py:16
  10.8 0.6 copy-done.10
  11.5 2.0 %scatter_fusion.2 = s32[128,2]{0,1:T(2,128)S(1)} fusion(s32[128,2]{0,1:T(2,128)S(1)} %broadcast.143.clone.1, s32[32]{0:T(128)S(1)} %get-tuple-element.47, s32[32]{0:T(128)S(1)} %bitcast.116), kind=kCustom, calls=%fused_computation.2 | custom fusion | bytes 640 | tf_op jit(solution)/shard_map/scatter | solution.py:44
  13.5 0.7 copy.30
  14.2 20.0 %all-to-all-start.2 = ((s32[128,1,2]{2,1,0:T(1,128)}), s32[128,1,2]{2,1,0:T(1,128)S(1)}, u32[]{:S(2)}, u32[]{:S(2)}) async-start(s32[128,1,2]{2,1,0:T(1,128)} %copy.30), calls=%async_computation.2 | async-start | bytes 131072 | tf_op jit(solution)/shard_map/all_to_all | solution.py:127
  34.2 0.6 copy-done.11
  35.0 0.6 convolution_bitcast_fusion.1
  35.6 0.7 fusion.3
  36.4 1.9 %scatter_fusion = f32[128,2,4,128]{3,2,1,0:T(4,128)S(1)} fusion(f32[128,2,4,128]{3,2,1,0:T(4,128)S(1)} %broadcast_in_dim.8, s32[32]{0:T(128)S(1)} %get-tuple-element.46, f32[32,4,128]{2,1,0:T(4,128)S(1)} %bitcast.105), kind=kCustom, calls=%fused_computation | custom fusion | bytes 196864 | tf_op jit(solution)/shard_map/scatter | solution.py:40
  38.3 2.1 %collective-permute-start.2 = (f32[128,2,4,128]{3,2,1,0:T(4,128)S(1)}, f32[128,2,4,128]{3,2,1,0:T(4,128)}, u32[]{:S(2)}, u32[]{:S(2)}) collective-permute-start(f32[128,2,4,128]{3,2,1,0:T(4,128)S(1)} %scatter_fusion), channel_id=1, source_target_pairs={{0,256},{128,384},{256,0},{384,128},{1,257},{129,385},{257,1},{385... | collective-permute-start | bytes 1572872 | tf_op jit(solution)/shard_map/ppermute | solution.py:16
  40.4 0.6 copy-done.12
  41.2 0.7 copy.26
  41.9 7.3 %all-to-all-done.2 = s32[128,1,2]{2,1,0:T(1,128)S(1)} async-done(((s32[128,1,2]{2,1,0:T(1,128)}), s32[128,1,2]{2,1,0:T(1,128)S(1)}, u32[]{:S(2)}, u32[]{:S(2)}) %all-to-all-start.2) | async-done | bytes 1056 | tf_op jit(solution)/shard_map/all_to_all | solution.py:127
  49.2 9.2 %all-to-all-start.1 = ((s32[128,1,2]{2,1,0:T(1,128)}), s32[128,1,2]{2,1,0:T(1,128)S(1)}, u32[]{:S(2)}, u32[]{:S(2)}) async-start(s32[128,1,2]{2,1,0:T(1,128)} %copy.26), calls=%async_computation.1 | async-start | bytes 131072 | tf_op jit(solution)/shard_map/all_to_all | solution.py:122
  58.4 0.3 fusion.20
  58.7 2.0 %scatter_fusion.3 = f32[128,2,128]{2,1,0:T(2,128)S(1)} fusion(f32[128,2,128]{2,1,0:T(2,128)S(1)} %broadcast_in_dim.10, s32[32]{0:T(128)S(1)} %get-tuple-element.47, f32[32,128]{1,0:T(8,128)S(1)} %bitcast.106), kind=kCustom, calls=%fused_computation.3 | custom fusion | bytes 49408 | tf_op jit(solution)/shard_map/scatter | solution.py:40
  60.8 12.6 %all-to-all-done.1 = s32[128,1,2]{2,1,0:T(1,128)S(1)} async-done(((s32[128,1,2]{2,1,0:T(1,128)}), s32[128,1,2]{2,1,0:T(1,128)S(1)}, u32[]{:S(2)}, u32[]{:S(2)}) %all-to-all-start.1) | async-done | bytes 1056 | tf_op jit(solution)/shard_map/all_to_all | solution.py:122
  73.3 23.9 %all_to_all.28 = f32[128,2,128]{2,1,0:T(2,128)} all-to-all(f32[128,2,128]{2,1,0:T(2,128)S(1)} %scatter_fusion.3), channel_id=1, replica_groups=mesh['sec'=4,'dom'=128] {'dom'}, dimensions={0} | all-to-all | bytes 262144 | tf_op jit(solution)/shard_map/all_to_all | solution.py:126
  97.3 7.2 %all-to-all-start = ((f32[128,2,4,128]{3,2,1,0:T(4,128)}), f32[128,2,4,128]{3,2,1,0:T(4,128)S(1)}, u32[]{:S(2)}, u32[]{:S(2)}) async-start(f32[128,2,4,128]{3,2,1,0:T(4,128)} %collective-permute-done.2), calls=%async_computation | async-start | bytes 1048576 | tf_op jit(solution)/shard_map/all_to_all | solution.py:121
  104.5 2.9 %collective-permute-start = (f32[30,1,128]{2,1,0:T(1,128)S(1)}, f32[30,1,128]{2,1,0:T(1,128)S(1)}, u32[]{:S(2)}, u32[]{:S(2)}) collective-permute-start(f32[30,1,128]{2,1,0:T(1,128)S(1)} %get-tuple-element.42), channel_id=1, source_target_pairs={{1,0},{2,1},{3,2},{4,3},{5,4},{6,5},{7,6},{8,7},{9,8},{10,9},{11,1... | collective-permute-start | bytes 46088 | tf_op jit(solution)/shard_map/ppermute | solution.py:29
  107.5 2.6 %collective-permute-start.1 = (f32[30,1,128]{2,1,0:T(1,128)S(1)}, f32[30,1,128]{2,1,0:T(1,128)S(1)}, u32[]{:S(2)}, u32[]{:S(2)}) collective-permute-start(f32[30,1,128]{2,1,0:T(1,128)S(1)} %get-tuple-element.43), channel_id=1, source_target_pairs={{0,1},{1,2},{2,3},{3,4},{4,5},{5,6},{6,7},{7,8},{8,9},{9,10},{10,1... | collective-permute-start | bytes 46088 | tf_op jit(solution)/shard_map/ppermute | solution.py:27
  110.1 0.2 fusion.48
  110.3 0.9 fusion.47
  111.2 0.5 broadcast.232
  111.8 0.8 reduce.11
  112.7 0.8 reduce.10
  113.7 14.1 %collective-permute-done = f32[30,1,128]{2,1,0:T(1,128)S(1)} collective-permute-done((f32[30,1,128]{2,1,0:T(1,128)S(1)}, f32[30,1,128]{2,1,0:T(1,128)S(1)}, u32[]{:S(2)}, u32[]{:S(2)}) %collective-permute-start) | collective-permute-done | bytes 15392 | tf_op jit(solution)/shard_map/ppermute | solution.py:29
  127.8 0.7 copy-done.8
  128.4 1.5 %fusion.19 = f32[30,32,128]{2,1,0:T(8,128)S(1)} fusion(f32[30,32,128]{2,1,0:T(8,128)S(1)} %bitcast.102, f32[30,1,128]{2,1,0:T(1,128)S(1)} %collective-permute-done.1, f32[30,1,128]{2,1,0:T(1,128)S(1)} %collective-permute-done, f32[30,32,127]{2,1,0:T(8,128)} %get-tuple-element.39, f32[30,32,1]{2,1,0:T(8,128)S(1)} %get-tuple-element.41, ...), kind=kLoop, calls=%fused_computation.30 | loop fusion | flops 1351680 | bytes 1996920 | tf_op jit(solution)/shard_map/add | solution.py:78
  130.0 0.9 fusion.1
  130.9 6.9 %all-to-all-done = f32[128,2,4,128]{3,2,1,0:T(4,128)S(1)} async-done(((f32[128,2,4,128]{3,2,1,0:T(4,128)}), f32[128,2,4,128]{3,2,1,0:T(4,128)S(1)}, u32[]{:S(2)}, u32[]{:S(2)}) %all-to-all-start) | async-done | bytes 524320 | tf_op jit(solution)/shard_map/all_to_all | solution.py:121
  137.8 0.3 copy.25
  138.1 0.3 fusion.23
  138.5 0.4 copy-done.3
  138.8 0.9 fusion.6
  139.8 0.3 copy.61
  140.1 0.2 fusion.45
  140.3 3.1 %collective-permute-start.4 = (f32[30,1,128]{2,1,0:T(1,128)S(1)}, f32[30,1,128]{2,1,0:T(1,128)S(1)}, u32[]{:S(2)}, u32[]{:S(2)}) collective-permute-start(f32[30,1,128]{2,1,0:T(1,128)S(1)} %get-tuple-element.36), channel_id=1, source_target_pairs={{1,0},{2,1},{3,2},{4,3},{5,4},{6,5},{7,6},{8,7},{9,8},{10,9},{11,1... | collective-permute-start | bytes 46088 | tf_op jit(solution)/shard_map/ppermute | solution.py:29
  143.4 3.6 %collective-permute-start.5 = (f32[30,1,128]{2,1,0:T(1,128)S(1)}, f32[30,1,128]{2,1,0:T(1,128)S(1)}, u32[]{:S(2)}, u32[]{:S(2)}) collective-permute-start(f32[30,1,128]{2,1,0:T(1,128)S(1)} %get-tuple-element.37), channel_id=1, source_target_pairs={{0,1},{1,2},{2,3},{3,4},{4,5},{5,6},{6,7},{7,8},{8,9},{9,10},{10,1... | collective-permute-start | bytes 46088 | tf_op jit(solution)/shard_map/ppermute | solution.py:27
  147.0 0.2 fusion.44
  147.2 0.6 collective-permute-done.5
  147.9 0.5 fusion.13
  148.4 0.9 convolution_bitcast_fusion
  149.4 1.1 copy.31
  (41 shorter events, 1.3 us)
Async XLA Ops:
  0.6 34.3 %copy-start = (f32[1,8,128,128]{3,2,1,0:T(8,128)S(1)}, f32[1,8,128,128]{3,2,1,0:T(8,128)}, u32[]{:S(2)}) copy-start(f32[1,8,128,128]{3,2,1,0:T(8,128)} %param.20) | copy-start | bytes 1572868
  0.6 0.7 copy-start.6
  1.7 0.7 copy-start.7
  2.7 0.7 copy-start.9
  5.3 35.8 %collective-permute-start.3 = (s32[128,2]{0,1:T(2,128)S(1)}, s32[128,2]{0,1:T(2,128)S(1)}, u32[]{:S(2)}, u32[]{:S(2)}) collective-permute-start(s32[128,2]{0,1:T(2,128)S(1)} %scatter_fusion.1), channel_id=1, source_target_pairs={{0,256},{128,384},{256,0},{384,128},{1,257},{129,385},{257,1},{385... | collective-permute-start | bytes 3080 | tf_op jit(solution)/shard_map/ppermute | solution.py:16
  10.8 0.7 copy-start.10
  11.5 23.5 %copy-start.1 = (f32[1,30,32,128]{3,2,1,0:T(8,128)S(1)}, f32[1,30,32,128]{3,2,1,0:T(8,128)}, u32[]{:S(2)}) copy-start(f32[1,30,32,128]{3,2,1,0:T(8,128)} %param.16) | copy-start | bytes 1474564
  14.2 35.0 %all-to-all-start.2 = ((s32[128,1,2]{2,1,0:T(1,128)}), s32[128,1,2]{2,1,0:T(1,128)S(1)}, u32[]{:S(2)}, u32[]{:S(2)}) async-start(s32[128,1,2]{2,1,0:T(1,128)} %copy.30), calls=%async_computation.2 | async-start | bytes 131072 | tf_op jit(solution)/shard_map/all_to_all | solution.py:127
  34.2 0.7 copy-start.11
  38.3 59.0 %collective-permute-start.2 = (f32[128,2,4,128]{3,2,1,0:T(4,128)S(1)}, f32[128,2,4,128]{3,2,1,0:T(4,128)}, u32[]{:S(2)}, u32[]{:S(2)}) collective-permute-start(f32[128,2,4,128]{3,2,1,0:T(4,128)S(1)} %scatter_fusion), channel_id=1, source_target_pairs={{0,256},{128,384},{256,0},{384,128},{1,257},{129,385},{257,1},{385... | collective-permute-start | bytes 1572872 | tf_op jit(solution)/shard_map/ppermute | solution.py:16
  40.4 0.7 copy-start.12
  49.2 24.1 %all-to-all-start.1 = ((s32[128,1,2]{2,1,0:T(1,128)}), s32[128,1,2]{2,1,0:T(1,128)S(1)}, u32[]{:S(2)}, u32[]{:S(2)}) async-start(s32[128,1,2]{2,1,0:T(1,128)} %copy.26), calls=%async_computation.1 | async-start | bytes 131072 | tf_op jit(solution)/shard_map/all_to_all | solution.py:122
  97.3 40.6 %all-to-all-start = ((f32[128,2,4,128]{3,2,1,0:T(4,128)}), f32[128,2,4,128]{3,2,1,0:T(4,128)S(1)}, u32[]{:S(2)}, u32[]{:S(2)}) async-start(f32[128,2,4,128]{3,2,1,0:T(4,128)} %collective-permute-done.2), calls=%async_computation | async-start | bytes 1048576 | tf_op jit(solution)/shard_map/all_to_all | solution.py:121
  104.5 23.2 %collective-permute-start = (f32[30,1,128]{2,1,0:T(1,128)S(1)}, f32[30,1,128]{2,1,0:T(1,128)S(1)}, u32[]{:S(2)}, u32[]{:S(2)}) collective-permute-start(f32[30,1,128]{2,1,0:T(1,128)S(1)} %get-tuple-element.42), channel_id=1, source_target_pairs={{1,0},{2,1},{3,2},{4,3},{5,4},{6,5},{7,6},{8,7},{9,8},{10,9},{11,1... | collective-permute-start | bytes 46088 | tf_op jit(solution)/shard_map/ppermute | solution.py:29
  107.5 20.3 %collective-permute-start.1 = (f32[30,1,128]{2,1,0:T(1,128)S(1)}, f32[30,1,128]{2,1,0:T(1,128)S(1)}, u32[]{:S(2)}, u32[]{:S(2)}) collective-permute-start(f32[30,1,128]{2,1,0:T(1,128)S(1)} %get-tuple-element.43), channel_id=1, source_target_pairs={{0,1},{1,2},{2,3},{3,4},{4,5},{5,6},{6,7},{7,8},{8,9},{9,10},{10,1... | collective-permute-start | bytes 46088 | tf_op jit(solution)/shard_map/ppermute | solution.py:27
  127.8 0.7 copy-start.8
  128.4 1.5 %copy-start.2 = (f32[128,2,128]{2,1,0:T(2,128)S(1)}, f32[128,2,128]{2,1,0:T(2,128)}, u32[]{:S(2)}) copy-start(f32[128,2,128]{2,1,0:T(2,128)} %all_to_all.28) | copy-start | bytes 393220
  128.4 1.6 %copy-start.4 = (f32[1,32,128]{2,1,0:T(8,128)S(1)}, f32[1,32,128]{2,1,0:T(8,128)}, u32[]{:S(2)}) copy-start(f32[1,32,128]{2,1,0:T(8,128)} %param.27) | copy-start | bytes 49156
  130.9 7.2 %copy-start.5 = (f32[1,32,128]{2,1,0:T(8,128)S(1)}, f32[1,32,128]{2,1,0:T(8,128)}, u32[]{:S(2)}) copy-start(f32[1,32,128]{2,1,0:T(8,128)} %param.17) | copy-start | bytes 49156
  138.1 0.7 copy-start.3
  140.3 6.9 %collective-permute-start.4 = (f32[30,1,128]{2,1,0:T(1,128)S(1)}, f32[30,1,128]{2,1,0:T(1,128)S(1)}, u32[]{:S(2)}, u32[]{:S(2)}) collective-permute-start(f32[30,1,128]{2,1,0:T(1,128)S(1)} %get-tuple-element.36), channel_id=1, source_target_pairs={{1,0},{2,1},{3,2},{4,3},{5,4},{6,5},{7,6},{8,7},{9,8},{10,9},{11,1... | collective-permute-start | bytes 46088 | tf_op jit(solution)/shard_map/ppermute | solution.py:29
  143.4 4.5 %collective-permute-start.5 = (f32[30,1,128]{2,1,0:T(1,128)S(1)}, f32[30,1,128]{2,1,0:T(1,128)S(1)}, u32[]{:S(2)}, u32[]{:S(2)}) collective-permute-start(f32[30,1,128]{2,1,0:T(1,128)S(1)} %get-tuple-element.37), channel_id=1, source_target_pairs={{0,1},{1,2},{2,3},{3,4},{4,5},{5,6},{6,7},{7,8},{8,9},{9,10},{10,1... | collective-permute-start | bytes 46088 | tf_op jit(solution)/shard_map/ppermute | solution.py:27
where the time goes:
time: 152 us; the launch traced here: 150 us
  starting transfers between devices  56.3 us (37%)
  waiting for transfers between devices  41.5 us (27%)
  blocking collectives  23.9 us (16%)
  local copies, waits for them, and re-layouts  18.5 us (12%)
  matrix products  4.74 us (3%)
  other arithmetic  4.48 us (3%)
    all_to_all x1, blocking collectives, shards(): lax.all_to_all(runoff_buffer, 'dom', split_axis=0, concat_axis=0, tiled=T...  23.9 us
    all_to_all x1, starting transfers between devices, shards(): lax.all_to_all(runoff_labels, 'dom', split_axis=0, concat_axis=0, tiled=T...  20 us
    ppermute x2, waiting for transfers between devices, with_halo(): lax.ppermute(head, axis, [((i + 1) % count, i) for i in range(ends)])  14.1 us
    all_to_all x1, waiting for transfers between devices, shards(): lax.all_to_all(moved[1], 'dom', split_axis=0, concat_axis=0, tiled=True)  12.6 us
    all_to_all x1, starting transfers between devices, shards(): lax.all_to_all(moved[1], 'dom', split_axis=0, concat_axis=0, tiled=True)  9.17 us
    ppermute x2, starting transfers between devices, partner(): return lax.ppermute(value, axis, pairs)  7.62 us
    all_to_all x1, waiting for transfers between devices, shards(): lax.all_to_all(runoff_labels, 'dom', split_axis=0, concat_axis=0, tiled=T...  7.3 us
    all_to_all x1, starting transfers between devices, shards(): lax.all_to_all(moved[0], 'dom', split_axis=0, concat_axis=0, tiled=True)  7.24 us
  transfers between devices with their start and end apart: 9, of which 5 were waited for; matrix products, arithmetic and copies ran while one was open for 10% of the time, Pallas kernels for 0%

commit v1 on v0

v1 whole, which is shorter than its diff:
```python
import jax
import jax.numpy as jnp
from jax import lax
from jax.experimental import pallas as pl
from jax.experimental.pallas import tpu as pltpu
from jax.sharding import PartitionSpec as P

MESH = pl.DeviceIdType.MESH
F32 = jnp.float32
BF16 = jnp.bfloat16

LEV = 30
PAD = 32
COLS = 128
ROWS = 32
FIELDS = 4
NW = 8
NY, NZ, NC = 4, 16, 2
N_DOM = NY * NZ * NC
GROUP = NY * NC
HALF = NZ // 2
SLOTS = NZ
GROUPS = ROWS // 8
MAIN = GROUP * ROWS
EDGE = GROUP * 2
LABELS = ROWS
FLUX = LABELS + 8
SLOT = FLUX + 2 * NC * ROWS
PARTS = [(0, FLUX)] + [(FLUX + i * ROWS, ROWS) for i in range(2 * NC)]
BLOCK = 2 * ROWS + 8


def tree(count, double):
    levels, reached, level = {}, 0, 1
    while reached < count:
        step = 2 if level in double and reached + 2 <= count else 1
        levels[level] = [(reached, reached + i) for i in range(step, 0, -1)]
        reached, level = reached + step, level + 1
    return levels


LONG, SHORT = tree(HALF, (1, 3, 5)), tree(HALF - 1, (2, 4))
LEVELS = len(LONG)


def split(x):
    high = x.astype(BF16)
    return high, (x - high.astype(F32)).astype(BF16)


def mm(a, b):
    return jnp.dot(a, b, preferred_element_type=F32)


def mm3(a, b):
    (ah, al), (bh, bl) = a, b
    return mm(ah, bh) + (mm(ah, bl) + mm(al, bh))


def iota(shape, dim):
    return lax.broadcasted_iota(jnp.int32, shape, dim)


def neighbours_in_columns(x):
    axis = x.ndim - 1
    return pltpu.roll(x, 1, axis) + pltpu.roll(x, COLS - 1, axis)


def laplacian(x, above, below):
    row, count = iota(x.shape, 1), x.shape[1]
    down = jnp.where(row == 0, above, pltpu.roll(x, 1, 1))
    up = jnp.where(row == count - 1, below, pltpu.roll(x, count - 1, 1))
    return down + up + neighbours_in_columns(x) - 4.0 * x


def kernel(
    state_h, frac_h, diff_h, ops_h, weight_h, fo_h, fr_h, fb_h, ro_h, rr_h, rb_h, store_h,
    base2, kab, forced, river,
    st, frac, diff, ops, weight, fo, fr, fb, ro, rr, rb, store,
    local_sem,
    hs_up, hs_dn, hr_up, hr_dn, halo_ssem, halo_rsem,
    terms, label_out, label_in, part_ssem, part_rsem,
    ring, ring_ssem, ring_rsem, row_of, ends_acc,
    flux_send, flux_recv, run_send, run_recv, rs_ssem, rs_rsem,
    dcol, kron_h, kron_l, base1,
):
    sec = lax.axis_index("sec")
    me = lax.axis_index("dom")
    core = me & (NC - 1)
    z = (me >> 1) & (NZ - 1)
    y = me >> 5

    def dom_of(yy, zz, cc):
        return (yy * NZ + zz) * NC + cc

    def along(distance):
        return (sec, dom_of(y, (z + NZ + distance) & (NZ - 1), core))

    partners = [(sec ^ 2, me), (sec ^ 2, me ^ 1)]
    after = (sec, (me + 1) & (N_DOM - 1))
    before = (sec, (me + N_DOM - 1) & (N_DOM - 1))

    def member(b):
        return (sec, dom_of((y + b // NC) & (NY - 1), z, core ^ (b % NC)))

    pairs = [(weight_h.at[0], weight)]
    pairs += [
        (state_h.at[0, :, pl.ds(8 * i, 8)], st.at[1 + i, pl.ds(0, LEV)]) for i in range(GROUPS)
    ]
    pairs += [
        (fb_h, fb), (rb_h, rb), (fo_h, fo), (fr_h, fr), (ro_h, ro), (rr_h, rr),
        (frac_h.at[0], frac), (ops_h, ops), (diff_h, diff), (store_h.at[0], store),
    ]
    loads = [pltpu.make_async_copy(a, b, local_sem.at[i]) for i, (a, b) in enumerate(pairs)]
    for copy in loads:
        copy.start()

    barrier = pltpu.get_barrier_semaphore()
    peers = [along(d) for d in (1, -1, 2, -2)] + [*partners, after, before] + [member(b) for b in range(1, GROUP)]
    for peer in peers:
        pl.semaphore_signal(barrier, inc=1, device_id=peer, device_id_type=MESH)

    for copy in loads[5:11]:
        copy.wait()

    def label_of(owner, row):
        eye = iota((ROWS, ROWS), 0) == iota((ROWS, ROWS), 1)
        target = (owner[...] * ROWS + row[...]).astype(F32)
        rows = jnp.broadcast_to(target, (ROWS, ROWS))
        column = jnp.sum(jnp.where(eye, rows, 0.0), axis=1, keepdims=True)
        wide = jnp.broadcast_to(column, (ROWS, COLS))
        place = iota((ROWS, COLS), 0) == (iota((ROWS, COLS), 1) & (ROWS - 1))
        return jnp.sum(jnp.where(place, wide, 0.0), axis=0, keepdims=True)

    label_out[...] = jnp.broadcast_to(label_of(fo, fr), (8, COLS))
    ring[0, LABELS:FLUX, :] = jnp.broadcast_to(label_of(ro, rr), (8, COLS))

    tall = FIELDS * ROWS + ROWS
    spot = (iota((tall, ROWS), 0) & (ROWS - 1)) == iota((tall, ROWS), 1)
    blocks = jnp.where(
        iota((tall, ROWS), 0) < FIELDS * ROWS,
        jnp.broadcast_to(fb[...].astype(F32), (tall, ROWS)),
        jnp.broadcast_to(rb[...].astype(F32), (tall, ROWS)),
    )
    block = jnp.sum(jnp.where(spot, blocks, 0.0), axis=1, keepdims=True)
    block = jnp.broadcast_to(jnp.concatenate([block, block], axis=0), (2 * tall, COLS))
    for copy in loads[1:5]:
        copy.wait()
    surface = jnp.concatenate(
        [st[1 + i, f] for f in (*range(FIELDS), 0) for i in range(GROUPS)], axis=0
    )
    high = surface.astype(BF16).astype(F32)
    both = jnp.concatenate([high, surface - high], axis=0)
    lhs = jnp.concatenate(
        [jnp.where(block == float(w), both, 0.0).astype(BF16) for w in range(NW)], axis=1
    )
    loads[0].wait()
    rhs = jnp.concatenate(split(weight[...].reshape(NW * COLS, COLS)), axis=1)
    total = mm(lhs, rhs)
    result = total[:tall, :COLS] + (total[:tall, COLS:] + total[tall:, :COLS])
    terms[...] = result[: FIELDS * ROWS].reshape(FIELDS, ROWS, COLS)
    ring[0, :LABELS, :] = result[FIELDS * ROWS :]

    pl.semaphore_wait(barrier, len(peers))

    def remote(src, dst, ssem, rsem, device):
        return pltpu.make_async_remote_copy(
            src_ref=src, dst_ref=dst, send_sem=ssem, recv_sem=rsem,
            device_id=device, device_id_type=MESH,
        )

    def slot_of(way, distance):
        return 0 if distance == 0 else min(2 * distance - (way > 0), SLOTS - 1)

    def hop(c, way, start, end):
        slot, rows = slot_of(way, end), pl.ds(*PARTS[c])
        return remote(
            ring.at[slot_of(way, start), rows], ring.at[slot, rows],
            ring_ssem.at[c, slot], ring_rsem.at[c, slot], along(way * (end - start)),
        )

    arrivals, departures = {}, {}
    for c in range(len(PARTS)):
        for way in (1, -1):
            levels = LONG if (c % 2 == 0) == (way > 0) else SHORT
            for level, edges in levels.items():
                copies = [hop(c, way, *edge) for edge in edges]
                departures[c, way, level] = (slot_of(way, edges[0][0]), copies)
                for copy, (_, end) in zip(copies, edges):
                    arrivals[c, slot_of(way, end)] = copy
    sends = list(arrivals.values())

    def arrive(c, slots):
        for slot in slots:
            if (c, slot) in arrivals:
                arrivals.pop((c, slot)).wait_recv()

    def depart(c, level):
        for way in (1, -1):
            if (c, way, level) in departures:
                slot, copies = departures.pop((c, way, level))
                arrive(c, [slot])
                for copy in copies:
                    copy.start()

    label_swap = [
        remote(label_out, label_in.at[i], part_ssem.at[i], part_rsem.at[i], to)
        for i, to in enumerate(partners)
    ]
    swap = []
    for c in range(1, len(PARTS)):
        i, f = (c - 1) // 2, (c - 1) % 2
        source = terms.at[2 * (core ^ i) + f]
        swap.append(
            remote(
                source, ring.at[0, pl.ds(*PARTS[c])],
                part_ssem.at[1 + c], part_rsem.at[1 + c], partners[i],
            )
        )
    for copy in (*label_swap, *swap):
        copy.start()

    loads[11].wait()
    hs_up[0:LEV] = st[1, 0:LEV, 0:2, :]
    hs_dn[0:LEV] = st[GROUPS, 0:LEV, 6:8, :]
    hs_up[LEV] = frac[0:2, :]
    hs_dn[LEV] = frac[ROWS - 2 : ROWS, :]
    hs_up[LEV + 1] = jnp.zeros((2, COLS), F32)
    hs_dn[LEV + 1] = jnp.zeros((2, COLS), F32)
    for i in range(GROUPS):
        st[1 + i, LEV:PAD] = jnp.zeros((PAD - LEV, 8, COLS), F32)
    halo = [
        remote(hs_dn, hr_up, halo_ssem.at[0], halo_rsem.at[0], after),
        remote(hs_up, hr_dn, halo_ssem.at[1], halo_rsem.at[1], before),
    ]
    for copy in halo:
        copy.start()

    tall8 = PAD * 8
    for copy in loads[12:14]:
        copy.wait()
    pick = ((iota((tall8, LEV), 0) >> 3) == iota((tall8, LEV), 1)).astype(F32)
    pick_t = ((iota((LEV, tall8), 1) >> 3) == iota((LEV, tall8), 0)).astype(BF16)
    column = jnp.sum(pick * jnp.broadcast_to(diff[...], (tall8, LEV)), axis=1, keepdims=True)
    dcol[...] = jnp.broadcast_to(column, (tall8, COLS))
    op = ops[:, 0, :]
    op_h, op_l = split(op)
    op_r = (op - op_h.astype(F32) - op_l.astype(F32)).astype(BF16)
    pick = pick.astype(BF16)
    spread = mm(mm(pick, op_h).astype(BF16), pick_t) + (
        mm(mm(pick, op_l).astype(BF16), pick_t) + mm(mm(pick, op_r).astype(BF16), pick_t)
    )
    same8 = (iota((tall8, tall8), 0) & 7) == (iota((tall8, tall8), 1) & 7)
    kh, kl = split(jnp.where(same8, spread, 0.0))
    kron_h[...] = kh
    kron_l[...] = kl

    def kab_work():
        k4 = kron_h[:, : 8 * FIELDS].astype(F32) + kron_l[:, : 8 * FIELDS].astype(F32)
        eye = (iota(k4.shape, 0) == iota(k4.shape, 1)).astype(F32)
        q = jnp.concatenate([k4 + eye, dcol[:, : 8 * FIELDS] * k4], axis=1)
        kh, kl = split(mm3((kron_h[...], kron_l[...]), split(q)))
        kab[...] = jnp.concatenate([kh, kh, kl], axis=1)

    def block_start(b):
        return dom_of((y + (b >> 1)) & (NY - 1), z, core ^ (b & 1)) * ROWS

    i = iota((MAIN, COLS), 0)
    row_of[:MAIN] = (block_start(i >> 5) + (i & (ROWS - 1))).astype(F32)
    i = iota((EDGE, COLS), 0)
    row_of[MAIN:] = (block_start(i >> 1) + jnp.where((i & 1) == 0, -1, ROWS)).astype(F32)
    flux_send[...] = jnp.zeros(flux_send.shape, F32)
    run_send[...] = jnp.zeros(run_send.shape, F32)

    first = me == 0
    last = me == N_DOM - 1

    def apply(*groups):
        u = jnp.concatenate([u.reshape(PAD * 8, COLS) for u in groups], axis=1)
        out = mm3((kron_h[...], kron_l[...]), split(u))
        return [
            out[:, COLS * i : COLS * (i + 1)].reshape(PAD, 8, COLS) for i in range(len(groups))
        ]

    def diffused(i, source):
        x = source[i]
        lap = laplacian(x, source[i - 1, :, 7:8], source[i + 1, :, 0:1])
        return x + dcol[...].reshape(PAD, 8, COLS) * lap

    def step_one(i, j):
        base1[i], base1[j] = apply(diffused(i, st), diffused(j, st))

    def step_two(i, j):
        base2[i - 1], base2[j - 1] = apply(diffused(i, base1), diffused(j, base1))

    def step_one_ends():
        d = dcol[...].reshape(PAD, 8, COLS)
        spot = iota((PAD, 8, COLS), 1)
        above, below = st[0], st[GROUPS + 1]
        x = jnp.where(spot == 7, above[:, 7:8], below[:, 0:1])
        outer = jnp.where(spot == 7, above[:, 6:7], below[:, 1:2])
        inner = jnp.where(spot == 7, st[1, :, 0:1], st[GROUPS, :, 7:8])
        u = x + d * (outer + inner + neighbours_in_columns(x) - 4.0 * x)
        gone = ((spot == 7) & first) | ((spot < 7) & last)
        (ends,) = apply(jnp.where(gone, 0.0, u))
        base1[0] = ends
        base1[GROUPS + 1] = ends

    for i, copy in enumerate(label_swap):
        copy.wait_recv()
        ring[0, LABELS + i : LABELS + i + 1, :] = label_in[i, 0:1, :]
    depart(0, 1)
    step_one(2, 3)
    for c in range(1, len(PARTS)):
        swap[c - 1].wait_recv()
        depart(c, 1)
    for copy in halo:
        copy.wait_recv()
    st[0, :, 6:8, :] = jnp.where(first, 0.0, hr_up[...])
    st[GROUPS + 1, :, 0:2, :] = jnp.where(last, 0.0, hr_dn[...])

    def joined(slot, picks):
        lane = iota((1, COLS), 1) >> 5
        names = None
        for i, (offset, row) in enumerate(picks):
            one = ring[slot + offset, LABELS + row : LABELS + row + 1, :]
            names = one if i == 0 else jnp.where(lane == i, one, names)
        return names

    def one_hot(rows, names):
        return (rows == jnp.broadcast_to(names, rows.shape)).astype(F32).astype(BF16)

    def place_flux(j):
        for c in range(len(PARTS)):
            arrive(c, (2 * j, 2 * j + 1))
        slot = 2 * j
        fields = [
            jnp.concatenate(
                [
                    ring[slot + s, FLUX + (2 * c + f) * ROWS : FLUX + (2 * c + f + 1) * ROWS, :]
                    for s in range(2)
                    for c in range(NC)
                ],
                axis=0,
            )
            for f in range(2)
        ]
        high, low = split(jnp.concatenate(fields, axis=1))
        sel = one_hot(row_of[...], joined(slot, [(0, 0), (0, 1), (1, 0), (1, 1)]))
        part = mm(jnp.concatenate([sel, sel], axis=1), jnp.concatenate([high, low], axis=0))
        for f in range(2):
            cells = slice(f * COLS, (f + 1) * COLS)
            rows = slice(f * ROWS, (f + 1) * ROWS)
            flux_send[:, rows, :] += part[:MAIN, cells].reshape(GROUP, ROWS, COLS)
        ends_acc[...] += part[MAIN:]

    def place_water(j):
        slot = 2 * j
        arrive(0, (slot, slot + 1))
        water = jnp.concatenate([ring[slot + s, :LABELS, :] for s in range(2)], axis=0)
        high, low = split(water)
        sel = one_hot(row_of[:MAIN], joined(slot, [(0, 2), (1, 2), (0, 2), (1, 2)]))
        part = mm(sel, jnp.concatenate([high, low], axis=0))
        run_send[...] += part.reshape(GROUP, ROWS, COLS)

    ends_acc[...] = jnp.zeros(ends_acc.shape, F32)

    work = {
        2: ([lambda: step_one(1, 4)], [lambda: place_water(0)]),
        3: ([lambda: place_flux(0)], [step_one_ends, lambda: place_water(1)]),
        4: (
            [lambda: place_flux(1)],
            [lambda: place_flux(2), lambda: place_water(2), lambda: place_water(3)],
        ),
        5: (
            [lambda: place_flux(3)],
            [lambda: place_flux(4), lambda: place_flux(5), lambda: place_water(4)],
        ),
    }
    for level in range(2, LEVELS + 1):
        for c in range(len(PARTS)):
            depart(c, level)
            if c == 2:
                for item in work[level][0]:
                    item()
        for item in work[level][1]:
            item()
    for j in (HALF - 3, HALF - 2, HALF - 1):
        place_water(j)

    order = [4, 5, 2, 3, 6, 7, 1]

    def scatter_copies(src, dst, c):
        return [
            remote(src.at[b], dst.at[b], rs_ssem.at[c, b], rs_rsem.at[c, b], member(b))
            for b in order
        ]

    flux_scatter = scatter_copies(flux_send, flux_recv, 1)
    water_scatter = scatter_copies(run_send, run_recv, 0)
    for copy in water_scatter:
        copy.start()
    place_flux(HALF - 2)
    place_flux(HALF - 1)
    for b in range(GROUP):
        for f in range(2):
            cells = slice(f * COLS, (f + 1) * COLS)
            ends = 2 * ROWS + 2 * f
            flux_send[b, ends : ends + 2, :] = ends_acc[2 * b : 2 * b + 2, cells]
    for copy in flux_scatter:
        copy.start()

    step_two(1, 2)
    step_two(3, 4)
    kab_work()
    for copy in (*label_swap, *swap, *halo, *sends):
        copy.wait_send()

    loads[14].wait()
    for copy in water_scatter:
        copy.wait_recv()
    water = run_send[0]
    for b in range(1, GROUP):
        water = water + run_recv[b]
    river[...] = store[...] + water

    for copy in flux_scatter:
        copy.wait_recv()

    same, other = flux_send[0], flux_recv[1]
    for b in range(2, GROUP, 2):
        same = same + flux_recv[b]
        other = other + flux_recv[b + 1]
    pair = [jnp.where(core == 0, same, other), jnp.where(core == 0, other, same)]

    g4 = jnp.stack(
        [frac[...] * pair[f // 2][(f % 2) * ROWS : (f % 2 + 1) * ROWS] for f in range(FIELDS)],
        axis=0,
    )
    ends = [pair[f // 2][2 * ROWS + 2 * (f % 2) : 2 * ROWS + 2 * (f % 2) + 2] for f in range(FIELDS)]
    frac_above = jnp.where(first, 0.0, hr_up[LEV, 1:2, :])
    frac_below = jnp.where(last, 0.0, hr_dn[LEV, 0:1, :])
    above = jnp.stack([frac_above * x[0:1] for x in ends], axis=0)
    below = jnp.stack([frac_below * x[1:2] for x in ends], axis=0)
    lap = laplacian(g4, above, below)
    for i in range(GROUPS):
        high, low = split(
            jnp.concatenate(
                [x[:, 8 * i : 8 * i + 8].reshape(8 * FIELDS, COLS) for x in (g4, lap)], axis=0
            )
        )
        forced[i] = jnp.concatenate([high, low, high], axis=0)

    for copy in (*flux_scatter, *water_scatter):
        copy.wait_send()


def finish(base2, kab, forced, river, out_h, river_h, out, sems):
    river_copy = pltpu.make_async_copy(river, river_h.at[0], sems.at[GROUPS])
    river_copy.start()
    copies = []
    for i in range(0, GROUPS, 2):
        delta = mm(kab[...], jnp.concatenate([forced[i], forced[i + 1]], axis=1))
        for j in range(2):
            part = delta[:, COLS * j : COLS * (j + 1)].reshape(PAD, 8, COLS)
            out[i + j] = base2[i + j] + part
            copies.append(
                pltpu.make_async_copy(
                    out.at[i + j, pl.ds(0, LEV)],
                    out_h.at[0, :, pl.ds(8 * (i + j), 8)],
                    sems.at[i + j],
                )
            )
            copies[-1].start()
    for copy in (*copies, river_copy):
        copy.wait()


def shards(
    state, frac, diff, ops, weight, fo, fr, fb, ro, rr, rb, store,
):
    ops = jnp.transpose(ops, (1, 0, 2))
    fo, ro = fo.reshape(1, ROWS), ro.reshape(1, ROWS)
    args = (state, frac, diff, ops, weight, fo, fr, fb, ro, rr, rb, store)
    args = [pltpu.with_memory_space_constraint(x, pltpu.HBM) for x in args]
    vmem = pltpu.VMEM
    far = pl.BlockSpec(memory_space=pltpu.HBM)
    near = pl.BlockSpec(memory_space=vmem)
    dma = pltpu.SemaphoreType.DMA
    i32 = jnp.int32
    inner = pl.pallas_call(
        kernel,
        out_shape=(
            vmem((GROUPS, PAD, 8, COLS), F32),
            vmem((PAD * 8, 3 * 16 * FIELDS), BF16),
            vmem((GROUPS, 3 * 16 * FIELDS, COLS), BF16),
            vmem((ROWS, COLS), F32),
        ),
        in_specs=[far] * 12,
        out_specs=(near,) * 4,
        scratch_shapes=[
            vmem((GROUPS + 2, PAD, 8, COLS), F32),
            vmem((ROWS, COLS), F32),
            vmem((1, LEV), F32),
            vmem((LEV, 1, LEV), F32),
            vmem((NW, COLS, COLS), F32),
            vmem((1, ROWS), i32),
            vmem((1, ROWS), i32),
            vmem((1, ROWS), i32),
            vmem((1, ROWS), i32),
            vmem((1, ROWS), i32),
            vmem((1, ROWS), i32),
            vmem((ROWS, COLS), F32),
            dma((15,)),
            vmem((PAD, 2, COLS), F32),
            vmem((PAD, 2, COLS), F32),
            vmem((PAD, 2, COLS), F32),
            vmem((PAD, 2, COLS), F32),
            dma((2,)),
            dma((2,)),
            vmem((FIELDS, ROWS, COLS), F32),
            vmem((8, COLS), F32),
            vmem((2, 8, COLS), F32),
            dma((len(PARTS) + 1,)),
            dma((len(PARTS) + 1,)),
            vmem((SLOTS, SLOT, COLS), F32),
            dma((len(PARTS), SLOTS)),
            dma((len(PARTS), SLOTS)),
            vmem((MAIN + EDGE, COLS), F32),
            vmem((EDGE, 2 * COLS), F32),
            vmem((GROUP, BLOCK, COLS), F32),
            vmem((GROUP, BLOCK, COLS), F32),
            vmem((GROUP, ROWS, COLS), F32),
            vmem((GROUP, ROWS, COLS), F32),
            dma((2, GROUP)),
            dma((2, GROUP)),
            vmem((PAD * 8, COLS), F32),
            vmem((PAD * 8, PAD * 8), BF16),
            vmem((PAD * 8, PAD * 8), BF16),
            vmem((GROUPS + 2, PAD, 8, COLS), F32),
        ],
        compiler_params=pltpu.CompilerParams(
            collective_id=0, has_side_effects=True, vmem_limit_bytes=32 * 1024 * 1024
        ),
        name="coupling",
    )(*args)
    inner = [pltpu.with_memory_space_constraint(x, vmem) for x in inner]
    return pl.pallas_call(
        finish,
        out_shape=(
            pltpu.HBM((1, LEV, ROWS, COLS), F32),
            pltpu.HBM((1, ROWS, COLS), F32),
        ),
        in_specs=[near] * 4,
        out_specs=(far, far),
        scratch_shapes=[vmem((GROUPS, PAD, 8, COLS), F32), dma((GROUPS + 1,))],
        compiler_params=pltpu.CompilerParams(vmem_limit_bytes=16 * 1024 * 1024),
        name="finish",
    )(*inner)


def solution(mesh):
    in_specs = (
        P("sec", None, "dom", None),
        P("sec", "dom", None),
        P("sec", None),
        P("sec", None, None),
        P("sec", "dom", None, None),
        P("sec", "dom", None),
        P("sec", "dom"),
        P("sec", "dom"),
        P("sec", "dom", None),
        P("sec", "dom"),
        P("sec", "dom"),
        P("sec", "dom", None),
    )
    out_specs = (P("sec", None, "dom", None), P("sec", "dom", None))
    return jax.shard_map(shards, mesh=mesh, in_specs=in_specs, out_specs=out_specs, check_vma=False)
```

time: 152 us -> 48.4 us (0.32)
  starting transfers between devices: 56.3 us -> 0 us
  Pallas kernels: 0 us -> 47.6 us
  waiting for transfers between devices: 41.5 us -> 0 us
  blocking collectives: 23.9 us -> 0 us
  local copies, waits for them, and re-layouts: 18.5 us -> 0 us
  matrix products: 4.74 us -> 0 us
  other arithmetic: 4.48 us -> 0 us
    pallas_call x0 -> x2, Pallas kernels: none -> 47.6 us  [the longest x1 46.5 us: shards(): pl.pallas_call(kernel, out_shape=(vmem((GROUPS, PAD, 8, COLS), F32), vmem...]
    all_to_all x3 -> x0, starting transfers between devices: 36.4 us -> none  [the longest x1 20 us: shards(): lax.all_to_all(runoff_labels, 'dom', split_axis=0, concat_axis=0, tiled=T...]
    all_to_all x3 -> x0, waiting for transfers between devices: 26.8 us -> none  [the longest x1 12.6 us: shards(): lax.all_to_all(moved[1], 'dom', split_axis=0, concat_axis=0, tiled=True)]
    all_to_all x1 -> x0, blocking collectives: 23.9 us -> none  [shards(): lax.all_to_all(runoff_buffer, 'dom', split_axis=0, concat_axis=0, tiled=T...]
    ppermute x6 -> x0, starting transfers between devices: 19.9 us -> none  [the longest x2 7.62 us: partner(): return lax.ppermute(value, axis, pairs)]
    ppermute x6 -> x0, waiting for transfers between devices: 14.8 us -> none  [the longest x2 14.1 us: with_halo(): lax.ppermute(head, axis, [((i + 1) % count, i) for i in range(ends)])]
    scatter x4 -> x0, local copies, waits for them, and re-layouts: 7.88 us -> none  [the longest x2 3.99 us: pack_slots(): labels = jnp.full((owner_count, slot_count), -1, jnp.int32).at[owner, slo...]
    unnamed x27 -> x0, local copies, waits for them, and re-layouts: 6.08 us -> none
  transfers between devices with their start and end apart: 9 -> 0, of which waited for: 5 -> 0; matrix products, arithmetic and copies ran while one was open for 10% -> 0% of each run, Pallas kernels for 0% -> 0%
where the time goes in v1:
time: 48.4 us; the launch traced here: 48.2 us
  Pallas kernels  47.6 us (98%)
  between operations  0.64 us (1%)
    pallas_call x1, Pallas kernels, shards(): pl.pallas_call(kernel, out_shape=(vmem((GROUPS, PAD, 8, COLS), F32), vmem...  46.5 us
    pallas_call x1, Pallas kernels, shards(): pl.pallas_call(finish, out_shape=(pltpu.HBM((1, LEV, ROWS, COLS), F32), p...  1.05 us

profile of v1, /device:TPU:1, one launch (start us, length us, event | category | flops | bytes accessed | tf_op | source)
XLA Modules:
  0.0 48.2 jit_solution(9191124613818988663)
XLA Ops:
  0.6 46.5 %coupling.1 = (f32[4,32,8,128]{3,2,1,0:T(8,128)S(1)}, bf16[256,192]{1,0:T(8,128)(2,1)S(1)}, bf16[4,192,128]{2,1,0:T(8,128)(2,1)S(1)}, f32[32,128]{1,0:T(8,128)S(1)}) custom-call(f32[1,30,32,128]{3,2,1,0:T(8,128)} %state_h.1, f32[1,32,128]{2,1,0:T(8,128)} %frac_h.1, f32[1,30]{1,0:T(1,128)} %diff_h.1, f32[30,1,30]{2,1,0:T(1,128)} %bitcast.3, ...), custom_call_target="tpu_custom_call" | custom-call | tf_op jit(solution)/shard_map/coupling/pallas_call | solution.py:491
  47.2 1.1 %finish.1 = (f32[1,30,32,128]{3,2,1,0:T(8,128)}, f32[1,32,128]{2,1,0:T(8,128)}) custom-call(f32[4,32,8,128]{3,2,1,0:T(8,128)S(1)} %get-tuple-element.6.base2, bf16[256,192]{1,0:T(8,128)(2,1)S(1)} %get-tuple-element.7.kab, bf16[4,192,128]{2,1,0:T(8,128)(2,1)S(1)} %get-tuple-element.8.forced, f32[32,128]{1,0:T(8,128)S(1)} %get-tuple-element.9.river), custom_call_target="tpu_custom_call" | custom-call | tf_op jit(solution)/shard_map/finish/pallas_call | solution.py:548

commit v2 on v1

--- a/solution.py
+++ b/solution.py
@@ -23,23 +23,22 @@
 GROUPS = ROWS // 8
 MAIN = GROUP * ROWS
 EDGE = GROUP * 2
-LABELS = ROWS
-FLUX = LABELS + 8
+FLUX = ROWS
 SLOT = FLUX + 2 * NC * ROWS
-PARTS = [(0, FLUX)] + [(FLUX + i * ROWS, ROWS) for i in range(2 * NC)]
+PIECES = 1 + 2 * NC
+FLUX_LABEL, WATER_LABEL = PIECES, PIECES + 1
 BLOCK = 2 * ROWS + 8
 
 
-def tree(count, double):
-    levels, reached, level = {}, 0, 1
-    while reached < count:
-        step = 2 if level in double and reached + 2 <= count else 1
-        levels[level] = [(reached, reached + i) for i in range(step, 0, -1)]
-        reached, level = reached + step, level + 1
+def tree(jumps):
+    levels, reached = {}, 0
+    for level, jump in enumerate(jumps, 1):
+        levels[level] = [(reached, reached + i) for i in range(jump, 0, -1)]
+        reached += jump
     return levels
 
 
-LONG, SHORT = tree(HALF, (1, 3, 5)), tree(HALF - 1, (2, 4))
+LONG, SHORT = tree((2, 1, 2, 1, 2)), tree((1, 2, 1, 2, 1))
 LEVELS = len(LONG)
 
 
@@ -80,7 +79,7 @@
     local_sem,
     hs_up, hs_dn, hr_up, hr_dn, halo_ssem, halo_rsem,
     terms, label_out, label_in, part_ssem, part_rsem,
-    ring, ring_ssem, ring_rsem, row_of, ends_acc,
+    ring, lab_f, lab_w, ring_ssem, ring_rsem, row_of, ends_acc,
     flux_send, flux_recv, run_send, run_recv, rs_ssem, rs_rsem,
     dcol, kron_h, kron_l, base1,
 ):
@@ -132,8 +131,8 @@
         place = iota((ROWS, COLS), 0) == (iota((ROWS, COLS), 1) & (ROWS - 1))
         return jnp.sum(jnp.where(place, wide, 0.0), axis=0, keepdims=True)
 
-    label_out[...] = jnp.broadcast_to(label_of(fo, fr), (8, COLS))
-    ring[0, LABELS:FLUX, :] = jnp.broadcast_to(label_of(ro, rr), (8, COLS))
+    label_out[...] = label_of(fo, fr)
+    lab_w[0] = label_of(ro, rr)
 
     tall = FIELDS * ROWS + ROWS
     spot = (iota((tall, ROWS), 0) & (ROWS - 1)) == iota((tall, ROWS), 1)
@@ -159,7 +158,7 @@
     total = mm(lhs, rhs)
     result = total[:tall, :COLS] + (total[:tall, COLS:] + total[tall:, :COLS])
     terms[...] = result[: FIELDS * ROWS].reshape(FIELDS, ROWS, COLS)
-    ring[0, :LABELS, :] = result[FIELDS * ROWS :]
+    ring[0, :FLUX, :] = result[FIELDS * ROWS :]
 
     pl.semaphore_wait(barrier, len(peers))
 
@@ -172,15 +171,20 @@
     def slot_of(way, distance):
         return 0 if distance == 0 else min(2 * distance - (way > 0), SLOTS - 1)
 
+    def piece(c, slot):
+        if c < PIECES:
+            return ring.at[slot, pl.ds(c * ROWS, ROWS)]
+        return (lab_f if c == FLUX_LABEL else lab_w).at[slot]
+
     def hop(c, way, start, end):
-        slot, rows = slot_of(way, end), pl.ds(*PARTS[c])
+        slot = slot_of(way, end)
         return remote(
-            ring.at[slot_of(way, start), rows], ring.at[slot, rows],
+            piece(c, slot_of(way, start)), piece(c, slot),
             ring_ssem.at[c, slot], ring_rsem.at[c, slot], along(way * (end - start)),
         )
 
     arrivals, departures = {}, {}
-    for c in range(len(PARTS)):
+    for c in range(PIECES + 2):
         for way in (1, -1):
             levels = LONG if (c % 2 == 0) == (way > 0) else SHORT
             for level, edges in levels.items():
@@ -208,17 +212,22 @@
         for i, to in enumerate(partners)
     ]
     swap = []
-    for c in range(1, len(PARTS)):
-        i, f = (c - 1) // 2, (c - 1) % 2
-        source = terms.at[2 * (core ^ i) + f]
+    for c in range(1, PIECES):
+        f, i = (c - 1) // NC, (c - 1) % NC
         swap.append(
             remote(
-                source, ring.at[0, pl.ds(*PARTS[c])],
+                terms.at[2 * (core ^ i) + f], piece(c, 0),
                 part_ssem.at[1 + c], part_rsem.at[1 + c], partners[i],
             )
         )
     for copy in (*label_swap, *swap):
         copy.start()
+
+    def depart_water(level):
+        depart(WATER_LABEL, level)
+        depart(0, level)
+
+    depart_water(1)
 
     loads[11].wait()
     hs_up[0:LEV] = st[1, 0:LEV, 0:2, :]
@@ -269,8 +278,7 @@
     row_of[:MAIN] = (block_start(i >> 5) + (i & (ROWS - 1))).astype(F32)
     i = iota((EDGE, COLS), 0)
     row_of[MAIN:] = (block_start(i >> 1) + jnp.where((i & 1) == 0, -1, ROWS)).astype(F32)
-    flux_send[...] = jnp.zeros(flux_send.shape, F32)
-    run_send[...] = jnp.zeros(run_send.shape, F32)
+    flux_send[:, 2 * ROWS + 4 :, :] = jnp.zeros((GROUP, 4, COLS), F32)
 
     first = me == 0
     last = me == N_DOM - 1
@@ -306,110 +314,106 @@
         base1[0] = ends
         base1[GROUPS + 1] = ends
 
+    depart_water(2)
+    step_one(2, 3)
     for i, copy in enumerate(label_swap):
         copy.wait_recv()
-        ring[0, LABELS + i : LABELS + i + 1, :] = label_in[i, 0:1, :]
-    depart(0, 1)
-    step_one(2, 3)
-    for c in range(1, len(PARTS)):
+        lab_f[0, i : i + 1, :] = label_in[i]
+    depart(FLUX_LABEL, 1)
+    for c in range(1, PIECES):
         swap[c - 1].wait_recv()
         depart(c, 1)
+    depart_water(3)
     for copy in halo:
         copy.wait_recv()
     st[0, :, 6:8, :] = jnp.where(first, 0.0, hr_up[...])
     st[GROUPS + 1, :, 0:2, :] = jnp.where(last, 0.0, hr_dn[...])
 
-    def joined(slot, picks):
+    def joined(rows):
         lane = iota((1, COLS), 1) >> 5
-        names = None
-        for i, (offset, row) in enumerate(picks):
-            one = ring[slot + offset, LABELS + row : LABELS + row + 1, :]
-            names = one if i == 0 else jnp.where(lane == i, one, names)
+        names = rows[0]
+        for i in range(1, 4):
+            names = jnp.where(lane == i, rows[i], names)
         return names
 
     def one_hot(rows, names):
         return (rows == jnp.broadcast_to(names, rows.shape)).astype(F32).astype(BF16)
 
-    def place_flux(j):
-        for c in range(len(PARTS)):
-            arrive(c, (2 * j, 2 * j + 1))
-        slot = 2 * j
-        fields = [
-            jnp.concatenate(
-                [
-                    ring[slot + s, FLUX + (2 * c + f) * ROWS : FLUX + (2 * c + f + 1) * ROWS, :]
-                    for s in range(2)
-                    for c in range(NC)
-                ],
-                axis=0,
+    def select_flux(j):
+        arrive(FLUX_LABEL, (2 * j, 2 * j + 1))
+        rows = [lab_f[2 * j + i // 2, i % 2 : i % 2 + 1, :] for i in range(4)]
+        return one_hot(row_of[...], joined(rows))
+
+    def rows_of(f, slots):
+        parts = []
+        for slot in slots:
+            for c in range(1 + NC * f, 1 + NC * (f + 1)):
+                arrive(c, [slot])
+                parts.append(ring[slot, c * ROWS : (c + 1) * ROWS, :])
+        return jnp.concatenate(parts, axis=0)
+
+    def place_flux(first_slot, last_slot, fields, fresh):
+        sel = [select_flux(j) for j in range(first_slot // 2, last_slot // 2)]
+        data = [rows_of(f, range(first_slot, last_slot)) for f in fields]
+        high, low = split(jnp.concatenate(data, axis=1))
+        part = mm(jnp.concatenate([*sel, *sel], axis=1), jnp.concatenate([high, low], axis=0))
+        for i, f in enumerate(fields):
+            one = part[:, i * COLS : (i + 1) * COLS]
+            rows = slice(f * ROWS, (f + 1) * ROWS)
+            main = one[:MAIN].reshape(GROUP, ROWS, COLS)
+            flux_send[:, rows, :] = main if fresh else flux_send[:, rows, :] + main
+            ends_acc[f] = one[MAIN:] if fresh else ends_acc[f] + one[MAIN:]
+
+    def place_water():
+        for c in (WATER_LABEL, 0):
+            arrive(c, range(SLOTS))
+        high, low = split(jnp.concatenate([ring[slot, :FLUX, :] for slot in range(SLOTS)], axis=0))
+        sel = [
+            one_hot(row_of[:MAIN], joined([lab_w[4 * g + i] for i in range(4)]))
+            for g in range(SLOTS // 4)
+        ]
+        part = mm(jnp.concatenate([*sel, *sel], axis=1), jnp.concatenate([high, low], axis=0))
+        run_send[...] = part.reshape(GROUP, ROWS, COLS)
+        for copy in water_scatter:
+            copy.start()
+
+    order = [4, 5, 2, 3, 6, 7, 1]
+
+    def scatter_copies(src, dst, c, rows):
+        return [
+            remote(
+                src.at[b, rows], dst.at[b, rows], rs_ssem.at[c, b], rs_rsem.at[c, b], member(b)
             )
-            for f in range(2)
-        ]
-        high, low = split(jnp.concatenate(fields, axis=1))
-        sel = one_hot(row_of[...], joined(slot, [(0, 0), (0, 1), (1, 0), (1, 1)]))
-        part = mm(jnp.concatenate([sel, sel], axis=1), jnp.concatenate([high, low], axis=0))
-        for f in range(2):
-            cells = slice(f * COLS, (f + 1) * COLS)
-            rows = slice(f * ROWS, (f + 1) * ROWS)
-            flux_send[:, rows, :] += part[:MAIN, cells].reshape(GROUP, ROWS, COLS)
-        ends_acc[...] += part[MAIN:]
-
-    def place_water(j):
-        slot = 2 * j
-        arrive(0, (slot, slot + 1))
-        water = jnp.concatenate([ring[slot + s, :LABELS, :] for s in range(2)], axis=0)
-        high, low = split(water)
-        sel = one_hot(row_of[:MAIN], joined(slot, [(0, 2), (1, 2), (0, 2), (1, 2)]))
-        part = mm(sel, jnp.concatenate([high, low], axis=0))
-        run_send[...] += part.reshape(GROUP, ROWS, COLS)
-
-    ends_acc[...] = jnp.zeros(ends_acc.shape, F32)
-
-    work = {
-        2: ([lambda: step_one(1, 4)], [lambda: place_water(0)]),
-        3: ([lambda: place_flux(0)], [step_one_ends, lambda: place_water(1)]),
-        4: (
-            [lambda: place_flux(1)],
-            [lambda: place_flux(2), lambda: place_water(2), lambda: place_water(3)],
-        ),
-        5: (
-            [lambda: place_flux(3)],
-            [lambda: place_flux(4), lambda: place_flux(5), lambda: place_water(4)],
-        ),
-    }
-    for level in range(2, LEVELS + 1):
-        for c in range(len(PARTS)):
-            depart(c, level)
-            if c == 2:
-                for item in work[level][0]:
-                    item()
-        for item in work[level][1]:
-            item()
-    for j in (HALF - 3, HALF - 2, HALF - 1):
-        place_water(j)
-
-    order = [4, 5, 2, 3, 6, 7, 1]
-
-    def scatter_copies(src, dst, c):
-        return [
-            remote(src.at[b], dst.at[b], rs_ssem.at[c, b], rs_rsem.at[c, b], member(b))
             for b in order
         ]
 
-    flux_scatter = scatter_copies(flux_send, flux_recv, 1)
-    water_scatter = scatter_copies(run_send, run_recv, 0)
-    for copy in water_scatter:
-        copy.start()
-    place_flux(HALF - 2)
-    place_flux(HALF - 1)
-    for b in range(GROUP):
-        for f in range(2):
-            cells = slice(f * COLS, (f + 1) * COLS)
-            ends = 2 * ROWS + 2 * f
-            flux_send[b, ends : ends + 2, :] = ends_acc[2 * b : 2 * b + 2, cells]
-    for copy in flux_scatter:
-        copy.start()
-
+    water_scatter = scatter_copies(run_send, run_recv, 0, pl.ds(0, ROWS))
+    flux_scatter = [
+        scatter_copies(flux_send, flux_recv, 1, pl.ds(0, ROWS)),
+        scatter_copies(flux_send, flux_recv, 2, pl.ds(ROWS, BLOCK - ROWS)),
+    ]
+
+    for level in range(2, LEVELS + 1):
+        depart(FLUX_LABEL, level)
+        for c in range(1, PIECES):
+            depart(c, level)
+        depart_water(level + 2)
+        if level == LEVELS - 1:
+            place_water()
+    place_flux(0, 8, (0, 1), True)
+    place_flux(8, 12, (0, 1), False)
+    for f in range(2):
+        place_flux(12, SLOTS, (f,), False)
+        if f == 1:
+            for b in range(GROUP):
+                for e in range(2):
+                    ends = 2 * ROWS + 2 * e
+                    flux_send[b, ends : ends + 2, :] = ends_acc[e, 2 * b : 2 * b + 2]
+        for copy in flux_scatter[f]:
+            copy.start()
+
+    step_one(1, 4)
+    step_one_ends()
     step_two(1, 2)
     step_two(3, 4)
     kab_work()
@@ -424,7 +428,7 @@
         water = water + run_recv[b]
     river[...] = store[...] + water
 
-    for copy in flux_scatter:
+    for copy in (*flux_scatter[0], *flux_scatter[1]):
         copy.wait_recv()
 
     same, other = flux_send[0], flux_recv[1]
@@ -451,7 +455,7 @@
         )
         forced[i] = jnp.concatenate([high, low, high], axis=0)
 
-    for copy in (*flux_scatter, *water_scatter):
+    for copy in (*flux_scatter[0], *flux_scatter[1], *water_scatter):
         copy.wait_send()
 
 
@@ -519,21 +523,23 @@
             dma((2,)),
             dma((2,)),
             vmem((FIELDS, ROWS, COLS), F32),
-            vmem((8, COLS), F32),
-            vmem((2, 8, COLS), F32),
-            dma((len(PARTS) + 1,)),
-            dma((len(PARTS) + 1,)),
+            vmem((1, COLS), F32),
+            vmem((2, 1, COLS), F32),
+            dma((PIECES + 1,)),
+            dma((PIECES + 1,)),
             vmem((SLOTS, SLOT, COLS), F32),
-            dma((len(PARTS), SLOTS)),
-            dma((len(PARTS), SLOTS)),
+            vmem((SLOTS, 2, COLS), F32),
+            vmem((SLOTS, 1, COLS), F32),
+            dma((PIECES + 2, SLOTS)),
+            dma((PIECES + 2, SLOTS)),
             vmem((MAIN + EDGE, COLS), F32),
-            vmem((EDGE, 2 * COLS), F32),
+            vmem((2, EDGE, COLS), F32),
             vmem((GROUP, BLOCK, COLS), F32),
             vmem((GROUP, BLOCK, COLS), F32),
             vmem((GROUP, ROWS, COLS), F32),
             vmem((GROUP, ROWS, COLS), F32),
-            dma((2, GROUP)),
-            dma((2, GROUP)),
+            dma((3, GROUP)),
+            dma((3, GROUP)),
             vmem((PAD * 8, COLS), F32),
             vmem((PAD * 8, PAD * 8), BF16),
             vmem((PAD * 8, PAD * 8), BF16),

time: 48.4 us -> 48.2 us (level)
  no operation moved by 1% of the time
where the time goes in v2:
time: 48.2 us; the launch traced here: 48.1 us
  Pallas kernels  47.5 us (99%)
  between operations  0.64 us (1%)
    pallas_call x1, Pallas kernels, shards(): pl.pallas_call(kernel, out_shape=(vmem((GROUPS, PAD, 8, COLS), F32), vmem...  46.4 us
    pallas_call x1, Pallas kernels, shards(): pl.pallas_call(finish, out_shape=(pltpu.HBM((1, LEV, ROWS, COLS), F32), p...  1.05 us

profile of v2, /device:TPU:1, one launch (start us, length us, event | category | flops | bytes accessed | tf_op | source)
XLA Modules:
  0.0 48.1 jit_solution(6139128403411058548)
XLA Ops:
  0.6 46.4 %coupling.1 = (f32[4,32,8,128]{3,2,1,0:T(8,128)S(1)}, bf16[256,192]{1,0:T(8,128)(2,1)S(1)}, bf16[4,192,128]{2,1,0:T(8,128)(2,1)S(1)}, f32[32,128]{1,0:T(8,128)S(1)}) custom-call(f32[1,30,32,128]{3,2,1,0:T(8,128)} %state_h.1, f32[1,32,128]{2,1,0:T(8,128)} %frac_h.1, f32[1,30]{1,0:T(1,128)} %diff_h.1, f32[30,1,30]{2,1,0:T(1,128)} %bitcast.3, ...), custom_call_target="tpu_custom_call" | custom-call | tf_op jit(solution)/shard_map/coupling/pallas_call | solution.py:495
  47.1 1.0 %finish.1 = (f32[1,30,32,128]{3,2,1,0:T(8,128)}, f32[1,32,128]{2,1,0:T(8,128)}) custom-call(f32[4,32,8,128]{3,2,1,0:T(8,128)S(1)} %get-tuple-element.6.base2, bf16[256,192]{1,0:T(8,128)(2,1)S(1)} %get-tuple-element.7.kab, bf16[4,192,128]{2,1,0:T(8,128)(2,1)S(1)} %get-tuple-element.8.forced, f32[32,128]{1,0:T(8,128)S(1)} %get-tuple-element.9.river), custom_call_target="tpu_custom_call" | custom-call | tf_op jit(solution)/shard_map/finish/pallas_call | solution.py:554

commit v3 on v2

--- a/solution.py
+++ b/solution.py
@@ -23,10 +23,16 @@
 GROUPS = ROWS // 8
 MAIN = GROUP * ROWS
 EDGE = GROUP * 2
-FLUX = ROWS
+WATER_LABEL = ROWS
+FLUX_LABEL = WATER_LABEL + 8
+FLUX = FLUX_LABEL + 8
 SLOT = FLUX + 2 * NC * ROWS
-PIECES = 1 + 2 * NC
-FLUX_LABEL, WATER_LABEL = PIECES, PIECES + 1
+WATER, FIELD_A, FIELD_B = range(3)
+PIECES = (
+    (0, FLUX_LABEL),
+    (FLUX_LABEL, 8 + NC * ROWS),
+    (FLUX + NC * ROWS, NC * ROWS),
+)
 BLOCK = 2 * ROWS + 8
 
 
@@ -38,8 +44,9 @@
     return levels
 
 
-LONG, SHORT = tree((2, 1, 2, 1, 2)), tree((1, 2, 1, 2, 1))
-LEVELS = len(LONG)
+WATER_TREES = tree((2, 1, 2, 1, 2)), tree((1, 2, 1, 2, 1))
+FLUX_TREES = tree((2, 2, 2, 2)), tree((1, 2, 2, 2))
+LEVELS = len(FLUX_TREES[0])
 
 
 def split(x):
@@ -79,7 +86,7 @@
     local_sem,
     hs_up, hs_dn, hr_up, hr_dn, halo_ssem, halo_rsem,
     terms, label_out, label_in, part_ssem, part_rsem,
-    ring, lab_f, lab_w, ring_ssem, ring_rsem, row_of, ends_acc,
+    ring, ring_ssem, ring_rsem, row_of, ends_acc,
     flux_send, flux_recv, run_send, run_recv, rs_ssem, rs_rsem,
     dcol, kron_h, kron_l, base1,
 ):
@@ -101,6 +108,12 @@
 
     def member(b):
         return (sec, dom_of((y + b // NC) & (NY - 1), z, core ^ (b % NC)))
+
+    barrier = pltpu.get_barrier_semaphore()
+    peers = [*partners, *[along(d) for d in (1, -1, 2, -2)], after, before]
+    peers += [member(b) for b in range(1, GROUP)]
+    for peer in peers:
+        pl.semaphore_signal(barrier, inc=1, device_id=peer, device_id_type=MESH)
 
     pairs = [(weight_h.at[0], weight)]
     pairs += [
@@ -114,11 +127,6 @@
     for copy in loads:
         copy.start()
 
-    barrier = pltpu.get_barrier_semaphore()
-    peers = [along(d) for d in (1, -1, 2, -2)] + [*partners, after, before] + [member(b) for b in range(1, GROUP)]
-    for peer in peers:
-        pl.semaphore_signal(barrier, inc=1, device_id=peer, device_id_type=MESH)
-
     for copy in loads[5:11]:
         copy.wait()
 
@@ -132,7 +140,8 @@
         return jnp.sum(jnp.where(place, wide, 0.0), axis=0, keepdims=True)
 
     label_out[...] = label_of(fo, fr)
-    lab_w[0] = label_of(ro, rr)
+    ring[0, WATER_LABEL:FLUX_LABEL, :] = jnp.broadcast_to(label_of(ro, rr), (8, COLS))
+    ring[0, FLUX_LABEL:FLUX, :] = jnp.zeros((8, COLS), F32)
 
     tall = FIELDS * ROWS + ROWS
     spot = (iota((tall, ROWS), 0) & (ROWS - 1)) == iota((tall, ROWS), 1)
@@ -158,76 +167,7 @@
     total = mm(lhs, rhs)
     result = total[:tall, :COLS] + (total[:tall, COLS:] + total[tall:, :COLS])
     terms[...] = result[: FIELDS * ROWS].reshape(FIELDS, ROWS, COLS)
-    ring[0, :FLUX, :] = result[FIELDS * ROWS :]
-
-    pl.semaphore_wait(barrier, len(peers))
-
-    def remote(src, dst, ssem, rsem, device):
-        return pltpu.make_async_remote_copy(
-            src_ref=src, dst_ref=dst, send_sem=ssem, recv_sem=rsem,
-            device_id=device, device_id_type=MESH,
-        )
-
-    def slot_of(way, distance):
-        return 0 if distance == 0 else min(2 * distance - (way > 0), SLOTS - 1)
-
-    def piece(c, slot):
-        if c < PIECES:
-            return ring.at[slot, pl.ds(c * ROWS, ROWS)]
-        return (lab_f if c == FLUX_LABEL else lab_w).at[slot]
-
-    def hop(c, way, start, end):
-        slot = slot_of(way, end)
-        return remote(
-            piece(c, slot_of(way, start)), piece(c, slot),
-            ring_ssem.at[c, slot], ring_rsem.at[c, slot], along(way * (end - start)),
-        )
-
-    arrivals, departures = {}, {}
-    for c in range(PIECES + 2):
-        for way in (1, -1):
-            levels = LONG if (c % 2 == 0) == (way > 0) else SHORT
-            for level, edges in levels.items():
-                copies = [hop(c, way, *edge) for edge in edges]
-                departures[c, way, level] = (slot_of(way, edges[0][0]), copies)
-                for copy, (_, end) in zip(copies, edges):
-                    arrivals[c, slot_of(way, end)] = copy
-    sends = list(arrivals.values())
-
-    def arrive(c, slots):
-        for slot in slots:
-            if (c, slot) in arrivals:
-                arrivals.pop((c, slot)).wait_recv()
-
-    def depart(c, level):
-        for way in (1, -1):
-            if (c, way, level) in departures:
-                slot, copies = departures.pop((c, way, level))
-                arrive(c, [slot])
-                for copy in copies:
-                    copy.start()
-
-    label_swap = [
-        remote(label_out, label_in.at[i], part_ssem.at[i], part_rsem.at[i], to)
-        for i, to in enumerate(partners)
-    ]
-    swap = []
-    for c in range(1, PIECES):
-        f, i = (c - 1) // NC, (c - 1) % NC
-        swap.append(
-            remote(
-                terms.at[2 * (core ^ i) + f], piece(c, 0),
-                part_ssem.at[1 + c], part_rsem.at[1 + c], partners[i],
-            )
-        )
-    for copy in (*label_swap, *swap):
-        copy.start()
-
-    def depart_water(level):
-        depart(WATER_LABEL, level)
-        depart(0, level)
-
-    depart_water(1)
+    ring[0, :WATER_LABEL, :] = result[FIELDS * ROWS :]
 
     loads[11].wait()
     hs_up[0:LEV] = st[1, 0:LEV, 0:2, :]
@@ -238,13 +178,6 @@
     hs_dn[LEV + 1] = jnp.zeros((2, COLS), F32)
     for i in range(GROUPS):
         st[1 + i, LEV:PAD] = jnp.zeros((PAD - LEV, 8, COLS), F32)
-    halo = [
-        remote(hs_dn, hr_up, halo_ssem.at[0], halo_rsem.at[0], after),
-        remote(hs_up, hr_dn, halo_ssem.at[1], halo_rsem.at[1], before),
-    ]
-    for copy in halo:
-        copy.start()
-
     tall8 = PAD * 8
     for copy in loads[12:14]:
         copy.wait()
@@ -264,21 +197,93 @@
     kron_h[...] = kh
     kron_l[...] = kl
 
+    def block_start(b):
+        return dom_of((y + (b >> 1)) & (NY - 1), z, core ^ (b & 1)) * ROWS
+
+    i = iota((MAIN, COLS), 0)
+    row_of[:MAIN] = (block_start(i >> 5) + (i & (ROWS - 1))).astype(F32)
+    i = iota((EDGE, COLS), 0)
+    row_of[MAIN:] = (block_start(i >> 1) + jnp.where((i & 1) == 0, -1, ROWS)).astype(F32)
+    flux_send[:, 2 * ROWS + 4 :, :] = jnp.zeros((GROUP, 4, COLS), F32)
+
+    pl.semaphore_wait(barrier, len(peers))
+
+    def remote(src, dst, ssem, rsem, device):
+        return pltpu.make_async_remote_copy(
+            src_ref=src, dst_ref=dst, send_sem=ssem, recv_sem=rsem,
+            device_id=device, device_id_type=MESH,
+        )
+
+    def slot_of(way, distance):
+        return 0 if distance == 0 else min(2 * distance - (way > 0), SLOTS - 1)
+
+    def piece(c, slot):
+        return ring.at[slot, pl.ds(*PIECES[c])]
+
+    def hop(c, way, start, end):
+        slot = slot_of(way, end)
+        return remote(
+            piece(c, slot_of(way, start)), piece(c, slot),
+            ring_ssem, ring_rsem.at[c, slot], along(way * (end - start)),
+        )
+
+    arrivals, departures = {}, {}
+    for c in range(len(PIECES)):
+        for way in (1, -1):
+            trees = WATER_TREES if c == WATER else FLUX_TREES
+            levels = trees[(c % 2 == 0) != (way > 0)]
+            for level, edges in levels.items():
+                copies = [hop(c, way, *edge) for edge in edges]
+                departures[c, way, level] = (slot_of(way, edges[0][0]), copies)
+                for copy, (_, end) in zip(copies, edges):
+                    arrivals[c, slot_of(way, end)] = copy
+
+    def arrive(c, slots):
+        for slot in slots:
+            if (c, slot) in arrivals:
+                arrivals.pop((c, slot)).wait_recv()
+
+    def depart(c, level):
+        for way in (1, -1):
+            if (c, way, level) in departures:
+                slot, copies = departures.pop((c, way, level))
+                arrive(c, [slot])
+                for copy in copies:
+                    copy.start()
+
+    label_swap = [
+        remote(label_out, label_in.at[i], part_ssem.at[i], part_rsem.at[i], to)
+        for i, to in enumerate(partners)
+    ]
+    swap = []
+    for f in range(2):
+        for i in range(NC):
+            n = NC * f + i
+            swap.append(
+                remote(
+                    terms.at[2 * (core ^ i) + f], ring.at[0, pl.ds(FLUX + n * ROWS, ROWS)],
+                    part_ssem.at[2 + n], part_rsem.at[2 + n], partners[i],
+                )
+            )
+    for copy in (*label_swap, *swap):
+        copy.start()
+
+    depart(WATER, 1)
+
+    halo = [
+        remote(hs_dn, hr_up, halo_ssem.at[0], halo_rsem.at[0], after),
+        remote(hs_up, hr_dn, halo_ssem.at[1], halo_rsem.at[1], before),
+    ]
+    for copy in halo:
+        copy.start()
+
+
     def kab_work():
         k4 = kron_h[:, : 8 * FIELDS].astype(F32) + kron_l[:, : 8 * FIELDS].astype(F32)
         eye = (iota(k4.shape, 0) == iota(k4.shape, 1)).astype(F32)
         q = jnp.concatenate([k4 + eye, dcol[:, : 8 * FIELDS] * k4], axis=1)
         kh, kl = split(mm3((kron_h[...], kron_l[...]), split(q)))
         kab[...] = jnp.concatenate([kh, kh, kl], axis=1)
-
-    def block_start(b):
-        return dom_of((y + (b >> 1)) & (NY - 1), z, core ^ (b & 1)) * ROWS
-
-    i = iota((MAIN, COLS), 0)
-    row_of[:MAIN] = (block_start(i >> 5) + (i & (ROWS - 1))).astype(F32)
-    i = iota((EDGE, COLS), 0)
-    row_of[MAIN:] = (block_start(i >> 1) + jnp.where((i & 1) == 0, -1, ROWS)).astype(F32)
-    flux_send[:, 2 * ROWS + 4 :, :] = jnp.zeros((GROUP, 4, COLS), F32)
 
     first = me == 0
     last = me == N_DOM - 1
@@ -314,20 +319,16 @@
         base1[0] = ends
         base1[GROUPS + 1] = ends
 
-    depart_water(2)
     step_one(2, 3)
+    depart(WATER, 2)
     for i, copy in enumerate(label_swap):
         copy.wait_recv()
-        lab_f[0, i : i + 1, :] = label_in[i]
-    depart(FLUX_LABEL, 1)
-    for c in range(1, PIECES):
-        swap[c - 1].wait_recv()
+        ring[0, FLUX_LABEL + i : FLUX_LABEL + i + 1, :] = label_in[i]
+    for c in (FIELD_A, FIELD_B):
+        for copy in swap[NC * (c - 1) : NC * c]:
+            copy.wait_recv()
         depart(c, 1)
-    depart_water(3)
-    for copy in halo:
-        copy.wait_recv()
-    st[0, :, 6:8, :] = jnp.where(first, 0.0, hr_up[...])
-    st[GROUPS + 1, :, 0:2, :] = jnp.where(last, 0.0, hr_dn[...])
+    depart(WATER, 3)
 
     def joined(rows):
         lane = iota((1, COLS), 1) >> 5
@@ -339,18 +340,25 @@
     def one_hot(rows, names):
         return (rows == jnp.broadcast_to(names, rows.shape)).astype(F32).astype(BF16)
 
+    selected = {}
+
     def select_flux(j):
-        arrive(FLUX_LABEL, (2 * j, 2 * j + 1))
-        rows = [lab_f[2 * j + i // 2, i % 2 : i % 2 + 1, :] for i in range(4)]
+        if j not in selected:
+            selected[j] = make_selection(j)
+        return selected[j]
+
+    def make_selection(j):
+        arrive(FIELD_A, (2 * j, 2 * j + 1))
+        rows = []
+        for i in range(4):
+            row = FLUX_LABEL + i % 2
+            rows.append(ring[2 * j + i // 2, row : row + 1, :])
         return one_hot(row_of[...], joined(rows))
 
     def rows_of(f, slots):
-        parts = []
-        for slot in slots:
-            for c in range(1 + NC * f, 1 + NC * (f + 1)):
-                arrive(c, [slot])
-                parts.append(ring[slot, c * ROWS : (c + 1) * ROWS, :])
-        return jnp.concatenate(parts, axis=0)
+        start = FLUX + f * NC * ROWS
+        arrive((FIELD_A, FIELD_B)[f], slots)
+        return jnp.concatenate([ring[n, start : start + NC * ROWS, :] for n in slots], axis=0)
 
     def place_flux(first_slot, last_slot, fields, fresh):
         sel = [select_flux(j) for j in range(first_slot // 2, last_slot // 2)]
@@ -365,12 +373,12 @@
             ends_acc[f] = one[MAIN:] if fresh else ends_acc[f] + one[MAIN:]
 
     def place_water():
-        for c in (WATER_LABEL, 0):
-            arrive(c, range(SLOTS))
-        high, low = split(jnp.concatenate([ring[slot, :FLUX, :] for slot in range(SLOTS)], axis=0))
+        arrive(WATER, range(SLOTS))
+        rows = [ring[slot, :WATER_LABEL, :] for slot in range(SLOTS)]
+        high, low = split(jnp.concatenate(rows, axis=0))
+        labels = [ring[slot, WATER_LABEL : WATER_LABEL + 1, :] for slot in range(SLOTS)]
         sel = [
-            one_hot(row_of[:MAIN], joined([lab_w[4 * g + i] for i in range(4)]))
-            for g in range(SLOTS // 4)
+            one_hot(row_of[:MAIN], joined(labels[4 * g : 4 * g + 4])) for g in range(SLOTS // 4)
         ]
         part = mm(jnp.concatenate([*sel, *sel], axis=1), jnp.concatenate([high, low], axis=0))
         run_send[...] = part.reshape(GROUP, ROWS, COLS)
@@ -381,29 +389,33 @@
 
     def scatter_copies(src, dst, c, rows):
         return [
-            remote(
-                src.at[b, rows], dst.at[b, rows], rs_ssem.at[c, b], rs_rsem.at[c, b], member(b)
-            )
+            remote(src.at[b, rows], dst.at[b, rows], rs_ssem.at[c], rs_rsem.at[c], member(b))
             for b in order
         ]
 
-    water_scatter = scatter_copies(run_send, run_recv, 0, pl.ds(0, ROWS))
-    flux_scatter = [
-        scatter_copies(flux_send, flux_recv, 1, pl.ds(0, ROWS)),
-        scatter_copies(flux_send, flux_recv, 2, pl.ds(ROWS, BLOCK - ROWS)),
+    def whole(src, dst, c, rows):
+        others = pl.ds(1, GROUP - 1)
+        return remote(
+            src.at[others, rows], dst.at[others, rows], rs_ssem.at[c], rs_rsem.at[c], member(1)
+        )
+
+    kinds = [
+        (run_send, run_recv, 0, pl.ds(0, ROWS)),
+        (flux_send, flux_recv, 1, pl.ds(0, ROWS)),
+        (flux_send, flux_recv, 2, pl.ds(ROWS, BLOCK - ROWS)),
     ]
+    water_scatter, *flux_scatter = [scatter_copies(*kind) for kind in kinds]
+    water_whole, *flux_whole = [whole(*kind) for kind in kinds]
 
     for level in range(2, LEVELS + 1):
-        depart(FLUX_LABEL, level)
-        for c in range(1, PIECES):
-            depart(c, level)
-        depart_water(level + 2)
-        if level == LEVELS - 1:
+        depart(FIELD_A, level)
+        depart(FIELD_B, level)
+        depart(WATER, level + 2)
+        if level == LEVELS:
             place_water()
-    place_flux(0, 8, (0, 1), True)
-    place_flux(8, 12, (0, 1), False)
+    place_flux(0, 10, (0, 1), True)
     for f in range(2):
-        place_flux(12, SLOTS, (f,), False)
+        place_flux(10, SLOTS, (f,), False)
         if f == 1:
             for b in range(GROUP):
                 for e in range(2):
@@ -412,23 +424,28 @@
         for copy in flux_scatter[f]:
             copy.start()
 
+    for copy in halo:
+        copy.wait_recv()
+    st[0, :, 6:8, :] = jnp.where(first, 0.0, hr_up[...])
+    st[GROUPS + 1, :, 0:2, :] = jnp.where(last, 0.0, hr_dn[...])
     step_one(1, 4)
     step_one_ends()
     step_two(1, 2)
     step_two(3, 4)
     kab_work()
-    for copy in (*label_swap, *swap, *halo, *sends):
+    for copy in (*label_swap, *swap, *halo):
         copy.wait_send()
+    every = ring.at[pl.ds(1, SLOTS - 1)]
+    remote(every, every, ring_ssem, ring_rsem.at[0, 0], along(1)).wait_send()
 
     loads[14].wait()
-    for copy in water_scatter:
-        copy.wait_recv()
+    water_whole.wait_recv()
     water = run_send[0]
     for b in range(1, GROUP):
         water = water + run_recv[b]
     river[...] = store[...] + water
 
-    for copy in (*flux_scatter[0], *flux_scatter[1]):
+    for copy in flux_whole:
         copy.wait_recv()
 
     same, other = flux_send[0], flux_recv[1]
@@ -455,7 +472,7 @@
         )
         forced[i] = jnp.concatenate([high, low, high], axis=0)
 
-    for copy in (*flux_scatter[0], *flux_scatter[1], *water_scatter):
+    for copy in (*flux_whole, water_whole):
         copy.wait_send()
 
 
@@ -525,21 +542,19 @@
             vmem((FIELDS, ROWS, COLS), F32),
             vmem((1, COLS), F32),
             vmem((2, 1, COLS), F32),
-            dma((PIECES + 1,)),
-            dma((PIECES + 1,)),
+            dma((2 + 2 * NC,)),
+            dma((2 + 2 * NC,)),
             vmem((SLOTS, SLOT, COLS), F32),
-            vmem((SLOTS, 2, COLS), F32),
-            vmem((SLOTS, 1, COLS), F32),
-            dma((PIECES + 2, SLOTS)),
-            dma((PIECES + 2, SLOTS)),
+            dma(()),
+            dma((len(PIECES), SLOTS)),
             vmem((MAIN + EDGE, COLS), F32),
             vmem((2, EDGE, COLS), F32),
             vmem((GROUP, BLOCK, COLS), F32),
             vmem((GROUP, BLOCK, COLS), F32),
             vmem((GROUP, ROWS, COLS), F32),
             vmem((GROUP, ROWS, COLS), F32),
-            dma((3, GROUP)),
-            dma((3, GROUP)),
+            dma((3,)),
+            dma((3,)),
             vmem((PAD * 8, COLS), F32),
             vmem((PAD * 8, PAD * 8), BF16),
             vmem((PAD * 8, PAD * 8), BF16),

time: 48.2 us -> 47.4 us (0.983)
  Pallas kernels: 47.5 us -> 46.6 us
    pallas_call x1, Pallas kernels: 46.4 us -> 45.6 us  [shards(): pl.pallas_call(kernel, out_shape=(vmem((GROUPS, PAD, 8, COLS), F32), vmem...]
where the time goes in v3:
time: 47.4 us; the launch traced here: 47.2 us
  Pallas kernels  46.6 us (98%)
  between operations  0.64 us (1%)
    pallas_call x1, Pallas kernels, shards(): pl.pallas_call(kernel, out_shape=(vmem((GROUPS, PAD, 8, COLS), F32), vmem...  45.6 us
    pallas_call x1, Pallas kernels, shards(): pl.pallas_call(finish, out_shape=(pltpu.HBM((1, LEV, ROWS, COLS), F32), p...  1.05 us

profile of v3, /device:TPU:1, one launch (start us, length us, event | category | flops | bytes accessed | tf_op | source)
XLA Modules:
  0.0 47.2 jit_solution(7514285271642487473)
XLA Ops:
  0.6 45.6 %coupling.1 = (f32[4,32,8,128]{3,2,1,0:T(8,128)S(1)}, bf16[256,192]{1,0:T(8,128)(2,1)S(1)}, bf16[4,192,128]{2,1,0:T(8,128)(2,1)S(1)}, f32[32,128]{1,0:T(8,128)S(1)}) custom-call(f32[1,30,32,128]{3,2,1,0:T(8,128)} %state_h.1, f32[1,32,128]{2,1,0:T(8,128)} %frac_h.1, f32[1,30]{1,0:T(1,128)} %diff_h.1, f32[30,1,30]{2,1,0:T(1,128)} %bitcast.3, ...), custom_call_target="tpu_custom_call" | custom-call | tf_op jit(solution)/shard_map/coupling/pallas_call | solution.py:512
  46.2 1.0 %finish.1 = (f32[1,30,32,128]{3,2,1,0:T(8,128)}, f32[1,32,128]{2,1,0:T(8,128)}) custom-call(f32[4,32,8,128]{3,2,1,0:T(8,128)S(1)} %get-tuple-element.6.base2, bf16[256,192]{1,0:T(8,128)(2,1)S(1)} %get-tuple-element.7.kab, bf16[4,192,128]{2,1,0:T(8,128)(2,1)S(1)} %get-tuple-element.8.forced, f32[32,128]{1,0:T(8,128)S(1)} %get-tuple-element.9.river), custom_call_target="tpu_custom_call" | custom-call | tf_op jit(solution)/shard_map/finish/pallas_call | solution.py:569

commit v4 on v3

--- a/solution.py
+++ b/solution.py
@@ -27,11 +27,11 @@
 FLUX_LABEL = WATER_LABEL + 8
 FLUX = FLUX_LABEL + 8
 SLOT = FLUX + 2 * NC * ROWS
-WATER, FIELD_A, FIELD_B = range(3)
+WATER, FLUX_PIECES = 0, (1, 2, 3, 4)
 PIECES = (
     (0, FLUX_LABEL),
-    (FLUX_LABEL, 8 + NC * ROWS),
-    (FLUX + NC * ROWS, NC * ROWS),
+    (FLUX_LABEL, 8 + ROWS),
+    *[(FLUX + n * ROWS, ROWS) for n in range(1, 2 * NC)],
 )
 BLOCK = 2 * ROWS + 8
 
@@ -169,6 +169,70 @@
     terms[...] = result[: FIELDS * ROWS].reshape(FIELDS, ROWS, COLS)
     ring[0, :WATER_LABEL, :] = result[FIELDS * ROWS :]
 
+    pl.semaphore_wait(barrier, len(peers))
+
+    def remote(src, dst, ssem, rsem, device):
+        return pltpu.make_async_remote_copy(
+            src_ref=src, dst_ref=dst, send_sem=ssem, recv_sem=rsem,
+            device_id=device, device_id_type=MESH,
+        )
+
+    def slot_of(way, distance):
+        return 0 if distance == 0 else min(2 * distance - (way > 0), SLOTS - 1)
+
+    def piece(c, slot):
+        return ring.at[slot, pl.ds(*PIECES[c])]
+
+    def hop(c, way, start, end):
+        slot = slot_of(way, end)
+        return remote(
+            piece(c, slot_of(way, start)), piece(c, slot),
+            ring_ssem, ring_rsem.at[c, slot], along(way * (end - start)),
+        )
+
+    arrivals, departures = {}, {}
+    for c in range(len(PIECES)):
+        for way in (1, -1):
+            trees = WATER_TREES if c == WATER else FLUX_TREES
+            levels = trees[(c % 2 == 0) != (way > 0)]
+            for level, edges in levels.items():
+                copies = [hop(c, way, *edge) for edge in edges]
+                departures[c, way, level] = (slot_of(way, edges[0][0]), copies)
+                for copy, (_, end) in zip(copies, edges):
+                    arrivals[c, slot_of(way, end)] = copy
+
+    def arrive(c, slots):
+        for slot in slots:
+            if (c, slot) in arrivals:
+                arrivals.pop((c, slot)).wait_recv()
+
+    def depart(c, level):
+        for way in (1, -1):
+            if (c, way, level) in departures:
+                slot, copies = departures.pop((c, way, level))
+                arrive(c, [slot])
+                for copy in copies:
+                    copy.start()
+
+    label_swap = [
+        remote(label_out, label_in.at[i], part_ssem.at[i], part_rsem.at[i], to)
+        for i, to in enumerate(partners)
+    ]
+    swap = []
+    for f in range(2):
+        for i in range(NC):
+            n = NC * f + i
+            swap.append(
+                remote(
+                    terms.at[2 * (core ^ i) + f], ring.at[0, pl.ds(FLUX + n * ROWS, ROWS)],
+                    part_ssem.at[2 + n], part_rsem.at[2 + n], partners[i],
+                )
+            )
+    for copy in (*label_swap, *swap):
+        copy.start()
+
+    depart(WATER, 1)
+
     loads[11].wait()
     hs_up[0:LEV] = st[1, 0:LEV, 0:2, :]
     hs_dn[0:LEV] = st[GROUPS, 0:LEV, 6:8, :]
@@ -178,6 +242,14 @@
     hs_dn[LEV + 1] = jnp.zeros((2, COLS), F32)
     for i in range(GROUPS):
         st[1 + i, LEV:PAD] = jnp.zeros((PAD - LEV, 8, COLS), F32)
+    halo = [
+        remote(hs_dn, hr_up, halo_ssem.at[0], halo_rsem.at[0], after),
+        remote(hs_up, hr_dn, halo_ssem.at[1], halo_rsem.at[1], before),
+    ]
+    for copy in halo:
+        copy.start()
+
+
     tall8 = PAD * 8
     for copy in loads[12:14]:
         copy.wait()
@@ -206,78 +278,6 @@
     row_of[MAIN:] = (block_start(i >> 1) + jnp.where((i & 1) == 0, -1, ROWS)).astype(F32)
     flux_send[:, 2 * ROWS + 4 :, :] = jnp.zeros((GROUP, 4, COLS), F32)
 
-    pl.semaphore_wait(barrier, len(peers))
-
-    def remote(src, dst, ssem, rsem, device):
-        return pltpu.make_async_remote_copy(
-            src_ref=src, dst_ref=dst, send_sem=ssem, recv_sem=rsem,
-            device_id=device, device_id_type=MESH,
-        )
-
-    def slot_of(way, distance):
-        return 0 if distance == 0 else min(2 * distance - (way > 0), SLOTS - 1)
-
-    def piece(c, slot):
-        return ring.at[slot, pl.ds(*PIECES[c])]
-
-    def hop(c, way, start, end):
-        slot = slot_of(way, end)
-        return remote(
-            piece(c, slot_of(way, start)), piece(c, slot),
-            ring_ssem, ring_rsem.at[c, slot], along(way * (end - start)),
-        )
-
-    arrivals, departures = {}, {}
-    for c in range(len(PIECES)):
-        for way in (1, -1):
-            trees = WATER_TREES if c == WATER else FLUX_TREES
-            levels = trees[(c % 2 == 0) != (way > 0)]
-            for level, edges in levels.items():
-                copies = [hop(c, way, *edge) for edge in edges]
-                departures[c, way, level] = (slot_of(way, edges[0][0]), copies)
-                for copy, (_, end) in zip(copies, edges):
-                    arrivals[c, slot_of(way, end)] = copy
-
-    def arrive(c, slots):
-        for slot in slots:
-            if (c, slot) in arrivals:
-                arrivals.pop((c, slot)).wait_recv()
-
-    def depart(c, level):
-        for way in (1, -1):
-            if (c, way, level) in departures:
-                slot, copies = departures.pop((c, way, level))
-                arrive(c, [slot])
-                for copy in copies:
-                    copy.start()
-
-    label_swap = [
-        remote(label_out, label_in.at[i], part_ssem.at[i], part_rsem.at[i], to)
-        for i, to in enumerate(partners)
-    ]
-    swap = []
-    for f in range(2):
-        for i in range(NC):
-            n = NC * f + i
-            swap.append(
-                remote(
-                    terms.at[2 * (core ^ i) + f], ring.at[0, pl.ds(FLUX + n * ROWS, ROWS)],
-                    part_ssem.at[2 + n], part_rsem.at[2 + n], partners[i],
-                )
-            )
-    for copy in (*label_swap, *swap):
-        copy.start()
-
-    depart(WATER, 1)
-
-    halo = [
-        remote(hs_dn, hr_up, halo_ssem.at[0], halo_rsem.at[0], after),
-        remote(hs_up, hr_dn, halo_ssem.at[1], halo_rsem.at[1], before),
-    ]
-    for copy in halo:
-        copy.start()
-
-
     def kab_work():
         k4 = kron_h[:, : 8 * FIELDS].astype(F32) + kron_l[:, : 8 * FIELDS].astype(F32)
         eye = (iota(k4.shape, 0) == iota(k4.shape, 1)).astype(F32)
@@ -324,9 +324,8 @@
     for i, copy in enumerate(label_swap):
         copy.wait_recv()
         ring[0, FLUX_LABEL + i : FLUX_LABEL + i + 1, :] = label_in[i]
-    for c in (FIELD_A, FIELD_B):
-        for copy in swap[NC * (c - 1) : NC * c]:
-            copy.wait_recv()
+    for c in FLUX_PIECES:
+        swap[c - 1].wait_recv()
         depart(c, 1)
     depart(WATER, 3)
 
@@ -348,7 +347,7 @@
         return selected[j]
 
     def make_selection(j):
-        arrive(FIELD_A, (2 * j, 2 * j + 1))
+        arrive(FLUX_PIECES[0], (2 * j, 2 * j + 1))
         rows = []
         for i in range(4):
             row = FLUX_LABEL + i % 2
@@ -357,7 +356,8 @@
 
     def rows_of(f, slots):
         start = FLUX + f * NC * ROWS
-        arrive((FIELD_A, FIELD_B)[f], slots)
+        for c in FLUX_PIECES[NC * f : NC * (f + 1)]:
+            arrive(c, slots)
         return jnp.concatenate([ring[n, start : start + NC * ROWS, :] for n in slots], axis=0)
 
     def place_flux(first_slot, last_slot, fields, fresh):
@@ -408,8 +408,8 @@
     water_whole, *flux_whole = [whole(*kind) for kind in kinds]
 
     for level in range(2, LEVELS + 1):
-        depart(FIELD_A, level)
-        depart(FIELD_B, level)
+        for c in FLUX_PIECES:
+            depart(c, level)
         depart(WATER, level + 2)
         if level == LEVELS:
             place_water()

time: 47.4 us -> 46.8 us (0.987)
  Pallas kernels: 46.6 us -> 46 us
    pallas_call x1, Pallas kernels: 45.6 us -> 45 us  [shards(): pl.pallas_call(kernel, out_shape=(vmem((GROUPS, PAD, 8, COLS), F32), vmem...]
where the time goes in v4:
time: 46.8 us; the launch traced here: 46.7 us
  Pallas kernels  46 us (98%)
  between operations  0.64 us (1%)
    pallas_call x1, Pallas kernels, shards(): pl.pallas_call(kernel, out_shape=(vmem((GROUPS, PAD, 8, COLS), F32), vmem...  45 us
    pallas_call x1, Pallas kernels, shards(): pl.pallas_call(finish, out_shape=(pltpu.HBM((1, LEV, ROWS, COLS), F32), p...  1.05 us

profile of v4, /device:TPU:1, one launch (start us, length us, event | category | flops | bytes accessed | tf_op | source)
XLA Modules:
  0.0 46.7 jit_solution(3128716067750233106)
XLA Ops:
  0.6 45.0 %coupling.1 = (f32[4,32,8,128]{3,2,1,0:T(8,128)S(1)}, bf16[256,192]{1,0:T(8,128)(2,1)S(1)}, bf16[4,192,128]{2,1,0:T(8,128)(2,1)S(1)}, f32[32,128]{1,0:T(8,128)S(1)}) custom-call(f32[1,30,32,128]{3,2,1,0:T(8,128)} %state_h.1, f32[1,32,128]{2,1,0:T(8,128)} %frac_h.1, f32[1,30]{1,0:T(1,128)} %diff_h.1, f32[30,1,30]{2,1,0:T(1,128)} %bitcast.3, ...), custom_call_target="tpu_custom_call" | custom-call | tf_op jit(solution)/shard_map/coupling/pallas_call | solution.py:512
  45.6 1.0 %finish.1 = (f32[1,30,32,128]{3,2,1,0:T(8,128)}, f32[1,32,128]{2,1,0:T(8,128)}) custom-call(f32[4,32,8,128]{3,2,1,0:T(8,128)S(1)} %get-tuple-element.6.base2, bf16[256,192]{1,0:T(8,128)(2,1)S(1)} %get-tuple-element.7.kab, bf16[4,192,128]{2,1,0:T(8,128)(2,1)S(1)} %get-tuple-element.8.forced, f32[32,128]{1,0:T(8,128)S(1)} %get-tuple-element.9.river), custom_call_target="tpu_custom_call" | custom-call | tf_op jit(solution)/shard_map/finish/pallas_call | solution.py:569

commit v5 on v4

--- a/solution.py
+++ b/solution.py
@@ -206,13 +206,20 @@
             if (c, slot) in arrivals:
                 arrivals.pop((c, slot)).wait_recv()
 
+    later = []
+
     def depart(c, level):
         for way in (1, -1):
             if (c, way, level) in departures:
                 slot, copies = departures.pop((c, way, level))
                 arrive(c, [slot])
-                for copy in copies:
-                    copy.start()
+                copies[0].start()
+                later.extend(copies[1:])
+
+    def flush(count=None):
+        for copy in later[:count]:
+            copy.start()
+        del later[:count]
 
     label_swap = [
         remote(label_out, label_in.at[i], part_ssem.at[i], part_rsem.at[i], to)
@@ -232,6 +239,7 @@
         copy.start()
 
     depart(WATER, 1)
+    flush()
 
     loads[11].wait()
     hs_up[0:LEV] = st[1, 0:LEV, 0:2, :]
@@ -321,13 +329,17 @@
 
     step_one(2, 3)
     depart(WATER, 2)
+    flush()
     for i, copy in enumerate(label_swap):
         copy.wait_recv()
         ring[0, FLUX_LABEL + i : FLUX_LABEL + i + 1, :] = label_in[i]
     for c in FLUX_PIECES:
         swap[c - 1].wait_recv()
+        before_this = len(later)
         depart(c, 1)
+        flush(before_this)
     depart(WATER, 3)
+    flush()
 
     def joined(rows):
         lane = iota((1, COLS), 1) >> 5
@@ -410,7 +422,9 @@
     for level in range(2, LEVELS + 1):
         for c in FLUX_PIECES:
             depart(c, level)
+        flush()
         depart(WATER, level + 2)
+        flush()
         if level == LEVELS:
             place_water()
     place_flux(0, 10, (0, 1), True)

time: 46.8 us -> 47.4 us (1.013)
  Pallas kernels: 46 us -> 46.6 us
    pallas_call x1, Pallas kernels: 45 us -> 45.6 us  [shards(): pl.pallas_call(kernel, out_shape=(vmem((GROUPS, PAD, 8, COLS), F32), vmem...]
where the time goes in v5:
time: 47.4 us; the launch traced here: 47.3 us
  Pallas kernels  46.6 us (98%)
  between operations  0.64 us (1%)
    pallas_call x1, Pallas kernels, shards(): pl.pallas_call(kernel, out_shape=(vmem((GROUPS, PAD, 8, COLS), F32), vmem...  45.6 us
    pallas_call x1, Pallas kernels, shards(): pl.pallas_call(finish, out_shape=(pltpu.HBM((1, LEV, ROWS, COLS), F32), p...  1.05 us

profile of v5, /device:TPU:1, one launch (start us, length us, event | category | flops | bytes accessed | tf_op | source)
XLA Modules:
  0.0 47.3 jit_solution(18204583370898182925)
XLA Ops:
  0.6 45.6 %coupling.1 = (f32[4,32,8,128]{3,2,1,0:T(8,128)S(1)}, bf16[256,192]{1,0:T(8,128)(2,1)S(1)}, bf16[4,192,128]{2,1,0:T(8,128)(2,1)S(1)}, f32[32,128]{1,0:T(8,128)S(1)}) custom-call(f32[1,30,32,128]{3,2,1,0:T(8,128)} %state_h.1, f32[1,32,128]{2,1,0:T(8,128)} %frac_h.1, f32[1,30]{1,0:T(1,128)} %diff_h.1, f32[30,1,30]{2,1,0:T(1,128)} %bitcast.3, ...), custom_call_target="tpu_custom_call" | custom-call | tf_op jit(solution)/shard_map/coupling/pallas_call | solution.py:526
  46.2 1.0 %finish.1 = (f32[1,30,32,128]{3,2,1,0:T(8,128)}, f32[1,32,128]{2,1,0:T(8,128)}) custom-call(f32[4,32,8,128]{3,2,1,0:T(8,128)S(1)} %get-tuple-element.6.base2, bf16[256,192]{1,0:T(8,128)(2,1)S(1)} %get-tuple-element.7.kab, bf16[4,192,128]{2,1,0:T(8,128)(2,1)S(1)} %get-tuple-element.8.forced, f32[32,128]{1,0:T(8,128)S(1)} %get-tuple-element.9.river), custom_call_target="tpu_custom_call" | custom-call | tf_op jit(solution)/shard_map/finish/pallas_call | solution.py:583

commit v6 on v4

--- a/solution.py
+++ b/solution.py
@@ -45,7 +45,7 @@
 
 
 WATER_TREES = tree((2, 1, 2, 1, 2)), tree((1, 2, 1, 2, 1))
-FLUX_TREES = tree((2, 2, 2, 2)), tree((1, 2, 2, 2))
+FLUX_TREES = WATER_TREES
 LEVELS = len(FLUX_TREES[0])
 
 
@@ -411,11 +411,11 @@
         for c in FLUX_PIECES:
             depart(c, level)
         depart(WATER, level + 2)
-        if level == LEVELS:
+        if level == LEVELS - 1:
             place_water()
-    place_flux(0, 10, (0, 1), True)
+    place_flux(0, 12, (0, 1), True)
     for f in range(2):
-        place_flux(10, SLOTS, (f,), False)
+        place_flux(12, SLOTS, (f,), False)
         if f == 1:
             for b in range(GROUP):
                 for e in range(2):

time: 46.8 us -> 47.7 us (1.019)
  Pallas kernels: 46 us -> 46.9 us
    pallas_call x1, Pallas kernels: 45 us -> 45.9 us  [shards(): pl.pallas_call(kernel, out_shape=(vmem((GROUPS, PAD, 8, COLS), F32), vmem...]
where the time goes in v6:
time: 47.7 us; the launch traced here: 47.6 us
  Pallas kernels  46.9 us (98%)
  between operations  0.64 us (1%)
    pallas_call x1, Pallas kernels, shards(): pl.pallas_call(kernel, out_shape=(vmem((GROUPS, PAD, 8, COLS), F32), vmem...  45.9 us
    pallas_call x1, Pallas kernels, shards(): pl.pallas_call(finish, out_shape=(pltpu.HBM((1, LEV, ROWS, COLS), F32), p...  1.05 us

profile of v6, /device:TPU:1, one launch (start us, length us, event | category | flops | bytes accessed | tf_op | source)
XLA Modules:
  0.0 47.6 jit_solution(8972891296399231546)
XLA Ops:
  0.6 45.9 %coupling.1 = (f32[4,32,8,128]{3,2,1,0:T(8,128)S(1)}, bf16[256,192]{1,0:T(8,128)(2,1)S(1)}, bf16[4,192,128]{2,1,0:T(8,128)(2,1)S(1)}, f32[32,128]{1,0:T(8,128)S(1)}) custom-call(f32[1,30,32,128]{3,2,1,0:T(8,128)} %state_h.1, f32[1,32,128]{2,1,0:T(8,128)} %frac_h.1, f32[1,30]{1,0:T(1,128)} %diff_h.1, f32[30,1,30]{2,1,0:T(1,128)} %bitcast.3, ...), custom_call_target="tpu_custom_call" | custom-call | tf_op jit(solution)/shard_map/coupling/pallas_call | solution.py:512
  46.5 1.0 %finish.1 = (f32[1,30,32,128]{3,2,1,0:T(8,128)}, f32[1,32,128]{2,1,0:T(8,128)}) custom-call(f32[4,32,8,128]{3,2,1,0:T(8,128)S(1)} %get-tuple-element.6.base2, bf16[256,192]{1,0:T(8,128)(2,1)S(1)} %get-tuple-element.7.kab, bf16[4,192,128]{2,1,0:T(8,128)(2,1)S(1)} %get-tuple-element.8.forced, f32[32,128]{1,0:T(8,128)S(1)} %get-tuple-element.9.river), custom_call_target="tpu_custom_call" | custom-call | tf_op jit(solution)/shard_map/finish/pallas_call | solution.py:569

commit v7 on v4

--- a/solution.py
+++ b/solution.py
@@ -24,15 +24,14 @@
 MAIN = GROUP * ROWS
 EDGE = GROUP * 2
 WATER_LABEL = ROWS
-FLUX_LABEL = WATER_LABEL + 8
-FLUX = FLUX_LABEL + 8
+FLUX = WATER_LABEL + 8
 SLOT = FLUX + 2 * NC * ROWS
 WATER, FLUX_PIECES = 0, (1, 2, 3, 4)
 PIECES = (
-    (0, FLUX_LABEL),
-    (FLUX_LABEL, 8 + ROWS),
-    *[(FLUX + n * ROWS, ROWS) for n in range(1, 2 * NC)],
+    (0, FLUX),
+    *[(FLUX + n * ROWS, ROWS) for n in range(2 * NC)],
 )
+FLUX_LABEL = len(PIECES)
 BLOCK = 2 * ROWS + 8
 
 
@@ -86,7 +85,7 @@
     local_sem,
     hs_up, hs_dn, hr_up, hr_dn, halo_ssem, halo_rsem,
     terms, label_out, label_in, part_ssem, part_rsem,
-    ring, ring_ssem, ring_rsem, row_of, ends_acc,
+    ring, names_in, ring_ssem, names_ssem, ring_rsem, row_of, ends_acc,
     flux_send, flux_recv, run_send, run_recv, rs_ssem, rs_rsem,
     dcol, kron_h, kron_l, base1,
 ):
@@ -140,8 +139,7 @@
         return jnp.sum(jnp.where(place, wide, 0.0), axis=0, keepdims=True)
 
     label_out[...] = label_of(fo, fr)
-    ring[0, WATER_LABEL:FLUX_LABEL, :] = jnp.broadcast_to(label_of(ro, rr), (8, COLS))
-    ring[0, FLUX_LABEL:FLUX, :] = jnp.zeros((8, COLS), F32)
+    ring[0, WATER_LABEL:FLUX, :] = jnp.broadcast_to(label_of(ro, rr), (8, COLS))
 
     tall = FIELDS * ROWS + ROWS
     spot = (iota((tall, ROWS), 0) & (ROWS - 1)) == iota((tall, ROWS), 1)
@@ -181,17 +179,18 @@
         return 0 if distance == 0 else min(2 * distance - (way > 0), SLOTS - 1)
 
     def piece(c, slot):
-        return ring.at[slot, pl.ds(*PIECES[c])]
+        return names_in.at[slot] if c == FLUX_LABEL else ring.at[slot, pl.ds(*PIECES[c])]
 
     def hop(c, way, start, end):
         slot = slot_of(way, end)
         return remote(
             piece(c, slot_of(way, start)), piece(c, slot),
-            ring_ssem, ring_rsem.at[c, slot], along(way * (end - start)),
+            names_ssem if c == FLUX_LABEL else ring_ssem, ring_rsem.at[c, slot],
+            along(way * (end - start)),
         )
 
     arrivals, departures = {}, {}
-    for c in range(len(PIECES)):
+    for c in range(len(PIECES) + 1):
         for way in (1, -1):
             trees = WATER_TREES if c == WATER else FLUX_TREES
             levels = trees[(c % 2 == 0) != (way > 0)]
@@ -323,7 +322,8 @@
     depart(WATER, 2)
     for i, copy in enumerate(label_swap):
         copy.wait_recv()
-        ring[0, FLUX_LABEL + i : FLUX_LABEL + i + 1, :] = label_in[i]
+        names_in[0, i : i + 1, :] = label_in[i]
+    depart(FLUX_LABEL, 1)
     for c in FLUX_PIECES:
         swap[c - 1].wait_recv()
         depart(c, 1)
@@ -347,11 +347,10 @@
         return selected[j]
 
     def make_selection(j):
-        arrive(FLUX_PIECES[0], (2 * j, 2 * j + 1))
+        arrive(FLUX_LABEL, (2 * j, 2 * j + 1))
         rows = []
         for i in range(4):
-            row = FLUX_LABEL + i % 2
-            rows.append(ring[2 * j + i // 2, row : row + 1, :])
+            rows.append(names_in[2 * j + i // 2, i % 2 : i % 2 + 1, :])
         return one_hot(row_of[...], joined(rows))
 
     def rows_of(f, slots):
@@ -408,7 +407,7 @@
     water_whole, *flux_whole = [whole(*kind) for kind in kinds]
 
     for level in range(2, LEVELS + 1):
-        for c in FLUX_PIECES:
+        for c in (FLUX_LABEL, *FLUX_PIECES):
             depart(c, level)
         depart(WATER, level + 2)
         if level == LEVELS:
@@ -437,6 +436,8 @@
         copy.wait_send()
     every = ring.at[pl.ds(1, SLOTS - 1)]
     remote(every, every, ring_ssem, ring_rsem.at[0, 0], along(1)).wait_send()
+    every = names_in.at[pl.ds(1, SLOTS - 1)]
+    remote(every, every, names_ssem, ring_rsem.at[0, 0], along(1)).wait_send()
 
     loads[14].wait()
     water_whole.wait_recv()
@@ -545,8 +546,10 @@
             dma((2 + 2 * NC,)),
             dma((2 + 2 * NC,)),
             vmem((SLOTS, SLOT, COLS), F32),
+            vmem((SLOTS, 2, COLS), F32),
             dma(()),
-            dma((len(PIECES), SLOTS)),
+            dma(()),
+            dma((len(PIECES) + 1, SLOTS)),
             vmem((MAIN + EDGE, COLS), F32),
             vmem((2, EDGE, COLS), F32),
             vmem((GROUP, BLOCK, COLS), F32),

time: 46.8 us -> 46.4 us (level)
  no operation moved by 1% of the time
where the time goes in v7:
time: 46.4 us; the launch traced here: 46.2 us
  Pallas kernels  45.6 us (98%)
  between operations  0.64 us (1%)
    pallas_call x1, Pallas kernels, shards(): pl.pallas_call(kernel, out_shape=(vmem((GROUPS, PAD, 8, COLS), F32), vmem...  44.5 us
    pallas_call x1, Pallas kernels, shards(): pl.pallas_call(finish, out_shape=(pltpu.HBM((1, LEV, ROWS, COLS), F32), p...  1.05 us

profile of v7, /device:TPU:1, one launch (start us, length us, event | category | flops | bytes accessed | tf_op | source)
XLA Modules:
  0.0 46.2 jit_solution(5874826999252103213)
XLA Ops:
  0.6 44.5 %coupling.1 = (f32[4,32,8,128]{3,2,1,0:T(8,128)S(1)}, bf16[256,192]{1,0:T(8,128)(2,1)S(1)}, bf16[4,192,128]{2,1,0:T(8,128)(2,1)S(1)}, f32[32,128]{1,0:T(8,128)S(1)}) custom-call(f32[1,30,32,128]{3,2,1,0:T(8,128)} %state_h.1, f32[1,32,128]{2,1,0:T(8,128)} %frac_h.1, f32[1,30]{1,0:T(1,128)} %diff_h.1, f32[30,1,30]{2,1,0:T(1,128)} %bitcast.3, ...), custom_call_target="tpu_custom_call" | custom-call | tf_op jit(solution)/shard_map/coupling/pallas_call | solution.py:513
  45.2 1.0 %finish.1 = (f32[1,30,32,128]{3,2,1,0:T(8,128)}, f32[1,32,128]{2,1,0:T(8,128)}) custom-call(f32[4,32,8,128]{3,2,1,0:T(8,128)S(1)} %get-tuple-element.6.base2, bf16[256,192]{1,0:T(8,128)(2,1)S(1)} %get-tuple-element.7.kab, bf16[4,192,128]{2,1,0:T(8,128)(2,1)S(1)} %get-tuple-element.8.forced, f32[32,128]{1,0:T(8,128)S(1)} %get-tuple-element.9.river), custom_call_target="tpu_custom_call" | custom-call | tf_op jit(solution)/shard_map/finish/pallas_call | solution.py:572

commit v8 on v7

--- a/solution.py
+++ b/solution.py
@@ -213,6 +213,27 @@
                 for copy in copies:
                     copy.start()
 
+    right_first = (z >= 2) & (z <= 9)
+
+    def depart_by_way(pieces, level):
+        steps = {1: [], -1: []}
+        for way in steps:
+            for c in pieces:
+                if (c, way, level) in departures:
+                    slot, copies = departures.pop((c, way, level))
+                    steps[way].append((arrivals.pop((c, slot), None), copies))
+
+        def run(ways):
+            for way in ways:
+                for arrival, copies in steps[way]:
+                    if arrival is not None:
+                        arrival.wait_recv()
+                    for copy in copies:
+                        copy.start()
+
+        pl.when(right_first)(lambda: run((1, -1)))
+        pl.when(jnp.logical_not(right_first))(lambda: run((-1, 1)))
+
     label_swap = [
         remote(label_out, label_in.at[i], part_ssem.at[i], part_rsem.at[i], to)
         for i, to in enumerate(partners)
@@ -407,8 +428,7 @@
     water_whole, *flux_whole = [whole(*kind) for kind in kinds]
 
     for level in range(2, LEVELS + 1):
-        for c in (FLUX_LABEL, *FLUX_PIECES):
-            depart(c, level)
+        depart_by_way((FLUX_LABEL, *FLUX_PIECES), level)
         depart(WATER, level + 2)
         if level == LEVELS:
             place_water()

time: 46.4 us -> 49 us (1.056)
  Pallas kernels: 45.6 us -> 48.2 us
    pallas_call x1, Pallas kernels: 44.5 us -> 47.2 us  [shards(): pl.pallas_call(kernel, out_shape=(vmem((GROUPS, PAD, 8, COLS), F32), vmem...]
where the time goes in v8:
time: 49 us; the launch traced here: 48.9 us
  Pallas kernels  48.2 us (98%)
  between operations  0.64 us (1%)
    pallas_call x1, Pallas kernels, shards(): pl.pallas_call(kernel, out_shape=(vmem((GROUPS, PAD, 8, COLS), F32), vmem...  47.2 us
    pallas_call x1, Pallas kernels, shards(): pl.pallas_call(finish, out_shape=(pltpu.HBM((1, LEV, ROWS, COLS), F32), p...  1.05 us

profile of v8, /device:TPU:1, one launch (start us, length us, event | category | flops | bytes accessed | tf_op | source)
XLA Modules:
  0.0 48.9 jit_solution(14228554019913009757)
XLA Ops:
  0.6 47.2 %coupling.1 = (f32[4,32,8,128]{3,2,1,0:T(8,128)S(1)}, bf16[256,192]{1,0:T(8,128)(2,1)S(1)}, bf16[4,192,128]{2,1,0:T(8,128)(2,1)S(1)}, f32[32,128]{1,0:T(8,128)S(1)}) custom-call(f32[1,30,32,128]{3,2,1,0:T(8,128)} %state_h.1, f32[1,32,128]{2,1,0:T(8,128)} %frac_h.1, f32[1,30]{1,0:T(1,128)} %diff_h.1, f32[30,1,30]{2,1,0:T(1,128)} %bitcast.3, ...), custom_call_target="tpu_custom_call" | custom-call | tf_op jit(solution)/shard_map/coupling/pallas_call | solution.py:533
  47.8 1.0 %finish.1 = (f32[1,30,32,128]{3,2,1,0:T(8,128)}, f32[1,32,128]{2,1,0:T(8,128)}) custom-call(f32[4,32,8,128]{3,2,1,0:T(8,128)S(1)} %get-tuple-element.6.base2, bf16[256,192]{1,0:T(8,128)(2,1)S(1)} %get-tuple-element.7.kab, bf16[4,192,128]{2,1,0:T(8,128)(2,1)S(1)} %get-tuple-element.8.forced, f32[32,128]{1,0:T(8,128)S(1)} %get-tuple-element.9.river), custom_call_target="tpu_custom_call" | custom-call | tf_op jit(solution)/shard_map/finish/pallas_call | solution.py:592

commit v9 on v7

--- a/solution.py
+++ b/solution.py
@@ -24,14 +24,14 @@
 MAIN = GROUP * ROWS
 EDGE = GROUP * 2
 WATER_LABEL = ROWS
-FLUX = WATER_LABEL + 8
+FLUX = WATER_LABEL
 SLOT = FLUX + 2 * NC * ROWS
 WATER, FLUX_PIECES = 0, (1, 2, 3, 4)
 PIECES = (
     (0, FLUX),
     *[(FLUX + n * ROWS, ROWS) for n in range(2 * NC)],
 )
-FLUX_LABEL = len(PIECES)
+FLUX_LABEL, WATER_NAMES = len(PIECES), len(PIECES) + 1
 BLOCK = 2 * ROWS + 8
 
 
@@ -85,7 +85,7 @@
     local_sem,
     hs_up, hs_dn, hr_up, hr_dn, halo_ssem, halo_rsem,
     terms, label_out, label_in, part_ssem, part_rsem,
-    ring, names_in, ring_ssem, names_ssem, ring_rsem, row_of, ends_acc,
+    ring, names_in, water_names, ring_ssem, names_ssem, water_ssem, ring_rsem, row_of, ends_acc,
     flux_send, flux_recv, run_send, run_recv, rs_ssem, rs_rsem,
     dcol, kron_h, kron_l, base1,
 ):
@@ -139,7 +139,7 @@
         return jnp.sum(jnp.where(place, wide, 0.0), axis=0, keepdims=True)
 
     label_out[...] = label_of(fo, fr)
-    ring[0, WATER_LABEL:FLUX, :] = jnp.broadcast_to(label_of(ro, rr), (8, COLS))
+    water_names[0] = label_of(ro, rr)
 
     tall = FIELDS * ROWS + ROWS
     spot = (iota((tall, ROWS), 0) & (ROWS - 1)) == iota((tall, ROWS), 1)
@@ -179,20 +179,22 @@
         return 0 if distance == 0 else min(2 * distance - (way > 0), SLOTS - 1)
 
     def piece(c, slot):
+        if c == WATER_NAMES:
+            return water_names.at[slot]
         return names_in.at[slot] if c == FLUX_LABEL else ring.at[slot, pl.ds(*PIECES[c])]
 
     def hop(c, way, start, end):
         slot = slot_of(way, end)
         return remote(
             piece(c, slot_of(way, start)), piece(c, slot),
-            names_ssem if c == FLUX_LABEL else ring_ssem, ring_rsem.at[c, slot],
+            {FLUX_LABEL: names_ssem, WATER_NAMES: water_ssem}.get(c, ring_ssem), ring_rsem.at[c, slot],
             along(way * (end - start)),
         )
 
     arrivals, departures = {}, {}
-    for c in range(len(PIECES) + 1):
+    for c in range(len(PIECES) + 2):
         for way in (1, -1):
-            trees = WATER_TREES if c == WATER else FLUX_TREES
+            trees = WATER_TREES if c in (WATER, WATER_NAMES) else FLUX_TREES
             levels = trees[(c % 2 == 0) != (way > 0)]
             for level, edges in levels.items():
                 copies = [hop(c, way, *edge) for edge in edges]
@@ -230,6 +232,7 @@
     for copy in (*label_swap, *swap):
         copy.start()
 
+    depart(WATER_NAMES, 1)
     depart(WATER, 1)
 
     loads[11].wait()
@@ -318,8 +321,9 @@
         base1[0] = ends
         base1[GROUPS + 1] = ends
 
+    depart(WATER_NAMES, 2)
+    depart(WATER, 2)
     step_one(2, 3)
-    depart(WATER, 2)
     for i, copy in enumerate(label_swap):
         copy.wait_recv()
         names_in[0, i : i + 1, :] = label_in[i]
@@ -327,6 +331,7 @@
     for c in FLUX_PIECES:
         swap[c - 1].wait_recv()
         depart(c, 1)
+    depart(WATER_NAMES, 3)
     depart(WATER, 3)
 
     def joined(rows):
@@ -372,10 +377,11 @@
             ends_acc[f] = one[MAIN:] if fresh else ends_acc[f] + one[MAIN:]
 
     def place_water():
+        arrive(WATER_NAMES, range(SLOTS))
         arrive(WATER, range(SLOTS))
         rows = [ring[slot, :WATER_LABEL, :] for slot in range(SLOTS)]
         high, low = split(jnp.concatenate(rows, axis=0))
-        labels = [ring[slot, WATER_LABEL : WATER_LABEL + 1, :] for slot in range(SLOTS)]
+        labels = [water_names[slot] for slot in range(SLOTS)]
         sel = [
             one_hot(row_of[:MAIN], joined(labels[4 * g : 4 * g + 4])) for g in range(SLOTS // 4)
         ]
@@ -409,6 +415,7 @@
     for level in range(2, LEVELS + 1):
         for c in (FLUX_LABEL, *FLUX_PIECES):
             depart(c, level)
+        depart(WATER_NAMES, level + 2)
         depart(WATER, level + 2)
         if level == LEVELS:
             place_water()
@@ -438,6 +445,8 @@
     remote(every, every, ring_ssem, ring_rsem.at[0, 0], along(1)).wait_send()
     every = names_in.at[pl.ds(1, SLOTS - 1)]
     remote(every, every, names_ssem, ring_rsem.at[0, 0], along(1)).wait_send()
+    every = water_names.at[pl.ds(1, SLOTS - 1)]
+    remote(every, every, water_ssem, ring_rsem.at[0, 0], along(1)).wait_send()
 
     loads[14].wait()
     water_whole.wait_recv()
@@ -547,9 +556,11 @@
             dma((2 + 2 * NC,)),
             vmem((SLOTS, SLOT, COLS), F32),
             vmem((SLOTS, 2, COLS), F32),
+            vmem((SLOTS, 1, COLS), F32),
             dma(()),
             dma(()),
-            dma((len(PIECES) + 1, SLOTS)),
+            dma(()),
+            dma((len(PIECES) + 2, SLOTS)),
             vmem((MAIN + EDGE, COLS), F32),
             vmem((2, EDGE, COLS), F32),
             vmem((GROUP, BLOCK, COLS), F32),

time: 46.4 us -> 46.1 us (level)
  no operation moved by 1% of the time
where the time goes in v9:
time: 46.1 us; the launch traced here: 46 us
  Pallas kernels  45.3 us (98%)
  between operations  0.64 us (1%)
    pallas_call x1, Pallas kernels, shards(): pl.pallas_call(kernel, out_shape=(vmem((GROUPS, PAD, 8, COLS), F32), vmem...  44.3 us
    pallas_call x1, Pallas kernels, shards(): pl.pallas_call(finish, out_shape=(pltpu.HBM((1, LEV, ROWS, COLS), F32), p...  1.05 us

profile of v9, /device:TPU:1, one launch (start us, length us, event | category | flops | bytes accessed | tf_op | source)
XLA Modules:
  0.0 46.0 jit_solution(10172027325873178390)
XLA Ops:
  0.6 44.3 %coupling.1 = (f32[4,32,8,128]{3,2,1,0:T(8,128)S(1)}, bf16[256,192]{1,0:T(8,128)(2,1)S(1)}, bf16[4,192,128]{2,1,0:T(8,128)(2,1)S(1)}, f32[32,128]{1,0:T(8,128)S(1)}) custom-call(f32[1,30,32,128]{3,2,1,0:T(8,128)} %state_h.1, f32[1,32,128]{2,1,0:T(8,128)} %frac_h.1, f32[1,30]{1,0:T(1,128)} %diff_h.1, f32[30,1,30]{2,1,0:T(1,128)} %bitcast.3, ...), custom_call_target="tpu_custom_call" | custom-call | tf_op jit(solution)/shard_map/coupling/pallas_call | solution.py:522
  44.9 1.0 %finish.1 = (f32[1,30,32,128]{3,2,1,0:T(8,128)}, f32[1,32,128]{2,1,0:T(8,128)}) custom-call(f32[4,32,8,128]{3,2,1,0:T(8,128)S(1)} %get-tuple-element.6.base2, bf16[256,192]{1,0:T(8,128)(2,1)S(1)} %get-tuple-element.7.kab, bf16[4,192,128]{2,1,0:T(8,128)(2,1)S(1)} %get-tuple-element.8.forced, f32[32,128]{1,0:T(8,128)S(1)} %get-tuple-element.9.river), custom_call_target="tpu_custom_call" | custom-call | tf_op jit(solution)/shard_map/finish/pallas_call | solution.py:583
